TPU v7x, 32 devices: a whole 2x2x4 slice. The times are simulated.
32 devices in a mesh: dp: 16 (over z, x, core), mp: 2 (over y).
Axes of the slice: x: 2, y: 2, z: 4, core: 2. Of those that a mesh axis runs over, the one named last changes fastest.
Arguments:
- tokens: bfloat16 [8192, 8192], P('dp', 'mp'), may hold values from -6 to 6
- upstream: bfloat16 [8192, 8192], P('dp', 'mp'), may hold values from -6 to 6
- first_factor: bfloat16 [32, 256, 256], P('mp', 'dp'), may hold values from -0.375 to 0.375
- second_factor: bfloat16 [32, 256, 256], P('mp', 'dp'), may hold values from -0.375 to 0.375
Outputs:
- mixed: bfloat16 [8192, 8192], P('dp', 'mp')
- grad_tokens: bfloat16 [8192, 8192], P('dp', 'mp')
- grad_first: float32 [32, 256, 256], P('mp', 'dp')
- grad_second: float32 [32, 256, 256], P('mp', 'dp')
All inputs are finite; a program needn't handle non-finite values.
Results may differ from a plain program's by a relative error of at most 0.0056.
Values may be sent and summed in bfloat16 or wider, within the bound.
No kernel may reach another device: no remote copies, remote signals or barrier semaphores. Data moves between devices by JAX's collectives and lax.ppermute only.
A program may use at most 128 MiB of HBM per device.

v0:
```python
import functools
import math

import jax
import jax.numpy as jnp
from jax import lax
from jax.experimental import pallas as pl
from jax.experimental.pallas import tpu as pltpu
from jax.sharding import PartitionSpec as P

BF16 = jnp.bfloat16
F32 = jnp.float32
ROOT_HALF = math.sqrt(0.5)
DENSITY = 1.0 / math.sqrt(2.0 * math.pi)
JOINED = (True, False, False, False)
TIES = {0: ((0, 2),), 1: ((1, 1),), 2: ((0, 3), (1, 3), (2, 2))}
VMEM = 20 * 1024 * 1024
LARGE = 1 << 20


def split_even(count, parts):
    parts = min(count, parts)
    edges = [count * step // parts for step in range(parts + 1)]
    return list(zip(edges[:-1], edges[1:]))


def split_by(count, weights):
    total, edges, run = sum(weights), [0], 0
    for weight in weights:
        run += weight
        edges.append(count * run // total)
    return [(lo, hi) for lo, hi in zip(edges[:-1], edges[1:]) if hi > lo]


def dot(left, right, left_dim, right_dim):
    return lax.dot_general(
        left, right, (((left_dim,), (right_dim,)), ((), ())), preferred_element_type=F32
    )


def aligned(index, size):
    return pl.ds(pl.multiple_of(index * size, size), size)


def placed_for(array):
    if array.ndim == 2 or array.ndim == 4 and array.size > LARGE:
        return pltpu.with_memory_space_constraint(array, pltpu.HBM)
    return array


def call(kernel, name, ids, grid, inputs, held, outputs, scratch=(), after=()):
    places = sorted(held)
    extra = [held[place] for place in places] + list(after)
    taken = len(inputs)

    def body(ids_ref, *refs):
        kernel(ids_ref, *refs[:taken], *refs[taken + len(extra) :])

    return pl.pallas_call(
        body,
        grid_spec=pltpu.PrefetchScalarGridSpec(
            num_scalar_prefetch=1,
            grid=grid,
            in_specs=[spec for _, spec in inputs] + [pl.BlockSpec(memory_space=pl.ANY)] * len(extra),
            out_specs=[spec for _, _, spec in outputs],
            scratch_shapes=list(scratch),
        ),
        out_shape=[jax.ShapeDtypeStruct(shape, dtype) for shape, dtype, _ in outputs],
        input_output_aliases={1 + taken + at: place for at, place in enumerate(places)},
        compiler_params=pltpu.CompilerParams(
            dimension_semantics=("arbitrary",) * len(grid), vmem_limit_bytes=VMEM
        ),
        cost_estimate=pl.CostEstimate(flops=1, bytes_accessed=1, transcendentals=0),
        name=name,
    )(ids, *[placed_for(array) for array, _ in inputs], *extra)


class Whole:
    def __init__(self, arrays, slots, relative, lanes=None):
        self.arrays, self.slots, self.relative = arrays, slots, relative
        self.cols, self.lane = lanes or (arrays[0].shape[3], 0)

    def specs(self, count, at):
        return [
            (
                array,
                pl.BlockSpec(
                    (array.shape[0], count, array.shape[2], self.cols),
                    lambda step, _: (0, at(step), 0, self.lane),
                ),
            )
            for array in self.arrays
        ]

    def load(self, refs, block, target, device):
        if not self.relative:
            return refs[0][:, block].reshape(target.shape)
        for ref, slots in zip(refs, self.slots):
            rows = ref.shape[2]
            for place, slot in enumerate(slots):
                target[aligned(lax.bitwise_xor(device, slot), rows), :] = ref[place, block]
        return target[...]


def combos(bits):
    found = [0]
    for bit in bits:
        found += [value | bit for value in found]
    return found


class Network:
    def __init__(self, size):
        bits = [1 << k for k in range(size.bit_length() - 1)]
        self.size = size
        self.near, self.far = bits[:2], bits[2:]
        self.rounds = [(bit,) for bit in bits]
        self.order = [0]
        for bits in reversed(self.rounds):
            self.order = [slot | mask for mask in combos(bits) for slot in self.order]

    def swap(self, array, mask):
        return lax.ppermute(array, "dp", [(at, at ^ mask) for at in range(self.size)])

    def gather(self, shard):
        combo = combos(self.far)
        first = [shard[None]] + [self.swap(shard[None], mask) for mask in combo[1:]]
        have = [(jnp.concatenate(first, axis=0), combo)]
        for mask in reversed(self.near):
            have = have + [(self.swap(array, mask), [slot | mask for slot in slots]) for array, slots in have]
        return Whole([array for array, _ in have], [slots for _, slots in have], True)

    def cut(self, slots, bits):
        mask = sum(bits)
        return [[slot for slot in slots if slot & mask == value] for value in combos(bits)]

    def first_cut(self):
        return self.cut(self.order, self.rounds[0])

    def scatter(self, parts, scale, joined=False):
        rounds = self.rounds[: len(self.near)] + [tuple(self.far)] if joined else self.rounds
        slots = self.first_cut()[0]
        terms, sends, marks = [parts[0]], parts[1:], []
        for step, bits in enumerate(rounds):
            marks.append(sends)
            terms += [self.swap(piece, mask) for piece, mask in zip(sends, combos(bits)[1:])]
            if step + 1 < len(rounds):
                lists = self.cut(slots, rounds[step + 1])
                spans = [(slots.index(members[0]), slots.index(members[-1]) + 1) for members in lists]
                sends = [sum(term[lo:hi].astype(F32) for term in terms).astype(BF16) for lo, hi in spans[1:]]
                terms = [term[spans[0][0] : spans[0][1]] for term in terms]
                slots = lists[0]
        result = sum(term[0].astype(F32) for term in terms) * scale
        return result, marks + [[result]]


def tiles(array, rows, cols, down, along, at):
    return [
        (
            array,
            pl.BlockSpec(
                (rows, cols),
                functools.partial(lambda row, col, step, _: (row, along * at(step) + col), row, col),
            ),
        )
        for row in range(down)
        for col in range(along)
    ]


def expand_kernel(weights, shifts, spans, group, inner, ids, *rest):
    x_refs, rest = rest[:2], rest[2:]
    w_refs, rest = rest[: len(weights.arrays)], rest[len(weights.arrays) :]
    outs, held = rest[:-1], rest[-1]
    blk = held.shape[1]
    halves = []
    for half in range(2):
        weight = weights.load(w_refs, half, held.at[half], ids[1])
        halves.append(dot(x_refs[half][...], weight, 1, 0).astype(BF16).T.astype(F32))
    width = blk // group
    for at, _ in enumerate(shifts):
        parts = [
            full[at * width : (at + 1) * width].reshape(width // inner, inner, -1) for full in halves
        ]
        piece = jnp.concatenate(parts, axis=1).astype(BF16)
        for place, (start, stop) in enumerate(spans):
            outs[at * len(spans) + place][...] = piece[start:stop]


def expand(ids, tokens, weights, shifts, spans, group, local, after=()):
    tok = tokens.shape[0]
    blk = tokens.shape[1] // local
    inner = blk // (local * group)
    cols = len(shifts) * (blk // group)
    shapes = [stop - start for _ in shifts for start, stop in spans]
    return call(
        functools.partial(expand_kernel, weights, shifts, spans, group, inner),
        "expand",
        ids,
        (local // 2,),
        tiles(tokens, tok, blk, 1, 2, lambda pair: pair)
        + weights.specs(2, lambda pair: pair),
        {},
        [
            (
                (count, local * inner, tok),
                BF16,
                pl.BlockSpec((count, 2 * inner, tok), lambda pair, _: (0, pair, 0)),
            )
            for count in shapes
        ],
        [pltpu.VMEM((2, blk, cols), BF16)],
        after,
    )


def order_matrix(blk, blocks, flip):
    inner = blk // blocks
    out = lax.broadcasted_iota(jnp.int32, (blk, blk), 1 if flip else 0)
    held = lax.broadcasted_iota(jnp.int32, (blk, blk), 0 if flip else 1)
    return (held == lax.rem(out, blocks) * inner + lax.div(out, blocks)).astype(F32).astype(BF16)


def store_term(term, slots_lists, relative, outs, scratch, device, block):
    if not relative:
        out = outs[0]
        out[:, block] = term.reshape(out.shape[0], out.shape[2], out.shape[3])
        return
    scratch[...] = term
    for out, slots in zip(outs, slots_lists):
        rows = out.shape[2]
        for place, slot in enumerate(slots):
            out[place, block] = scratch[aligned(lax.bitwise_xor(device, slot), rows), :].astype(out.dtype)


def mix_kernel(weights, cut, relative, group, blocks, backs, ids, own_ref, *rest):
    arrived, rest = rest[: group - 1], rest[group - 1 :]
    w_refs, rest = rest[: len(weights.arrays)], rest[len(weights.arrays) :]
    step = (len(rest) - 6 - len(cut) - len(backs) * (group - 1)) // 2
    x_refs, up_refs, rest = rest[:step], rest[step : 2 * step], rest[2 * step :]
    mixed_ref, back_own_ref = rest[:2]
    term_refs, rest = rest[2 : 2 + len(cut)], rest[2 + len(cut) :]
    back_refs, (moved, back, held, term) = rest[:-4], rest[-4:]
    me = ids[0]
    blk = held.shape[1]
    rows = blk // group
    there = order_matrix(blk, blocks, False)
    again = order_matrix(blk, blocks, True)
    for j in range(held.shape[0]):
        cols = slice(j * blk, (j + 1) * blk)
        moved[j, aligned(me, rows), :] = own_ref[j]
        for shift in range(1, group):
            moved[j, aligned(lax.rem(me - shift + group, group), rows), :] = arrived[shift - 1][j]
        weight = weights.load(w_refs, j, held.at[j], ids[1])
        ordered = dot(there, moved[j], 1, 0).astype(BF16)
        inner_out = dot(ordered.T, weight, 1, 0)
        cdf = 0.5 + 0.5 * lax.erf(inner_out * ROOT_HALF)
        mixed_ref[:, cols] = (x_refs[j][...].astype(F32) + inner_out * cdf).astype(BF16)
        slope = cdf + inner_out * (DENSITY * jnp.exp(-0.5 * inner_out * inner_out))
        grad_out = (up_refs[j][...].astype(F32) * slope).astype(BF16)
        store_term(dot(ordered, grad_out, 1, 0), cut, relative, term_refs, term.at[j], ids[1], j)
        returned = dot(weight, grad_out, 1, 1).astype(BF16)
        back[j] = dot(again, returned, 1, 0).astype(BF16)
        back_own_ref[j] = back[j, aligned(me, rows), :]
        for shift in range(1, group):
            piece = back[j, aligned(lax.rem(me + shift, group), rows), :]
            for at, (start, stop) in enumerate(backs):
                back_refs[(shift - 1) * len(backs) + at][j] = piece[start:stop]


def mix(ids, own, arrived, weights, tokens, upstream, held, span, group, local, cut, relative, term, backs):
    tok = tokens.shape[0]
    blk = tokens.shape[1] // local
    feat = blk // group
    per = feat // local
    first, last = span
    rows = blk // sum(len(slots) for slots in cut)
    step = math.gcd(2, math.gcd(first, last))
    lane = pl.BlockSpec((tok, step * blk), lambda j, _: (0, first // step + j))
    at = pl.BlockSpec((step, feat, tok), lambda j, _: (first // step + j, 0, 0))
    keys = ["mixed", "own"]
    outs = [(tokens.shape, BF16, lane), ((local, feat, tok), BF16, at)]
    term_key, (term_first, term_last) = term
    for place, slots in enumerate(cut):
        keys.append((term_key, place))
        outs.append(
            (
                (len(slots), term_last - term_first, rows, blk),
                F32 if place == 0 else BF16,
                pl.BlockSpec((len(slots), step, rows, blk), lambda j, _: (0, (first - term_first) // step + j, 0, 0)),
            )
        )
    for shift in range(1, group):
        for key, (b_first, b_last), (j_first, j_last) in backs:
            keys.append((key, shift))
            outs.append(
                (
                    (j_last - j_first, (b_last - b_first) * per, tok),
                    BF16,
                    pl.BlockSpec(
                        (step, (b_last - b_first) * per, tok),
                        functools.partial(lambda start, j, _: (start + j, 0, 0), (first - j_first) // step),
                    ),
                )
            )
    kept = {place: held[key] for place, key in enumerate(keys) if key in held}
    cuts = [(b_first * per, b_last * per) for _, (b_first, b_last), _ in backs]
    got = call(
        functools.partial(mix_kernel, weights, cut, relative, group, local * group, cuts),
        "mix",
        ids,
        ((last - first) // step,),
        [(own, at)]
        + [(array, pl.BlockSpec((step, feat, tok), lambda j, _: (j, 0, 0))) for array in arrived]
        + weights.specs(step, lambda j: first // step + j)
        + tiles(tokens, tok, blk, 1, step, lambda j: first // step + j)
        + tiles(upstream, tok, blk, 1, step, lambda j: first // step + j),
        kept,
        outs,
        [
            pltpu.VMEM((step, blk, tok), BF16),
            pltpu.VMEM((step, blk, tok), BF16),
            pltpu.VMEM((step, blk, blk), BF16),
            pltpu.VMEM((step, blk, blk), F32),
        ],
    )
    held.update(zip(keys, got))


def fold_kernel(columns, cut, relative, group, inner, pieces, ids, own_ref, *rest):
    arrived, rest = rest[: pieces * (group - 1)], rest[pieces * (group - 1) :]
    x_refs, up_refs, rest = rest[:2], rest[2:4], rest[4:]
    w_refs = []
    for weights in columns:
        w_refs.append(rest[: len(weights.arrays)])
        rest = rest[len(weights.arrays) :]
    out_ref, term_refs = rest[0], rest[1:-4]
    inner_grad, held, sorted_term, term = rest[-4:]
    me = ids[0]
    blk = held.shape[2]
    width = blk // group
    for shift in range(group):
        if shift == 0:
            piece = own_ref[...]
        else:
            refs = arrived[(shift - 1) * pieces : shift * pieces]
            piece = jnp.concatenate([ref[...] for ref in refs], axis=0)
        piece = piece.astype(F32)
        for half in range(2):
            part = piece[:, half * inner : (half + 1) * inner].reshape(width, -1)
            inner_grad[half, shift * width : (shift + 1) * width, :] = part.astype(BF16)
    for half in range(2):
        cols = slice(half * blk, (half + 1) * blk)
        if len(columns) == 1:
            weight = columns[0].load(w_refs[0], half, held.at[half], ids[1])
        else:
            start = 0
            for weights, refs in zip(columns, w_refs):
                size = weights.cols
                part = held.at[half, :, start : start + size]
                part[...] = weights.load(refs, half, part, ids[1])
                start += size
            weight = held[half]
        du = inner_grad[half]
        unsorted = dot(du, x_refs[half][...], 1, 0)
        for shift in range(group):
            source = lax.rem(me - shift + group, group)
            sorted_term[half, aligned(source, width), :] = unsorted[shift * width : (shift + 1) * width]
        store_term(sorted_term[half].T, cut, relative, term_refs, term.at[half], ids[1], half)
        back = dot(du.T, weight, 1, 1)
        out_ref[:, cols] = (up_refs[half][...].astype(F32) + back).astype(BF16)


def fold(ids, own, arrived, tokens, upstream, columns, grad_tokens, span, group, local, cut, relative, after):
    tok = tokens.shape[0]
    blk = tokens.shape[1] // local
    inner = blk // (local * group)
    first, last = span
    rows = blk // sum(len(slots) for slots in cut)
    start = first // 2
    lane = pl.BlockSpec((tok, 2 * blk), lambda pair, _: (0, start + pair))
    inputs = []
    for array, begin in [(own, 0)] + arrived:
        at = functools.partial(lambda skip, pair, _: (0, skip + pair, 0), start - begin // 2)
        inputs.append((array, pl.BlockSpec((array.shape[0], 2 * inner, tok), at)))
    for array in (tokens, upstream):
        inputs += tiles(array, tok, blk, 1, 2, lambda pair: start + pair)
    for weights in columns:
        inputs += weights.specs(2, lambda pair: start + pair)
    outs = [(tokens.shape, BF16, lane)] + [
        (
            (len(slots), last - first, rows, blk),
            F32 if place == 0 else BF16,
            pl.BlockSpec((len(slots), 2, rows, blk), lambda pair, _: (0, pair, 0, 0)),
        )
        for place, slots in enumerate(cut)
    ]
    pieces = len(arrived) // (group - 1)
    held = {} if grad_tokens is None else {0: grad_tokens}
    return call(
        functools.partial(fold_kernel, columns, cut, relative, group, inner, pieces),
        "fold",
        ids,
        ((last - first) // 2,),
        inputs,
        held,
        outs,
        [
            pltpu.VMEM((2, blk, tok), BF16),
            pltpu.VMEM((2, blk, blk), BF16),
            pltpu.VMEM((2, blk, blk), F32),
            pltpu.VMEM((2, blk, blk), F32),
        ],
        after,
    )


def send(array, shift, group):
    return lax.ppermute(array, "mp", [(at, (at + shift) % group) for at in range(group)])


def gather_plain(shard):
    local, rows, blk = shard.shape
    whole = lax.all_gather(shard, "dp", axis=0, tiled=False)
    if rows % 16:
        whole = jnp.transpose(whole, (1, 0, 2, 3)).reshape(1, local, whole.shape[0] * rows, blk)
    return Whole([whole], [list(range(whole.shape[0]))], False)


def scatter_plain(term, rows, scale):
    if term.shape[2] != rows:
        _, count, whole, blk = term.shape
        term = jnp.transpose(term.reshape(count, whole // rows, rows, blk), (1, 0, 2, 3))
    return lax.psum_scatter(term, "dp", scatter_dimension=0, tiled=False) * scale


def on_device(tokens, upstream, first_factor, second_factor):
    local, rows, blk = first_factor.shape
    group, size = lax.axis_size("mp"), lax.axis_size("dp")
    width = blk // group
    scale = 1.0 / math.sqrt(tokens.shape[0] * size)
    me, device = lax.axis_index("mp"), lax.axis_index("dp")
    ids = jnp.stack([me, device]).astype(jnp.int32)
    cube = group == 2 and size >= 8 and size & (size - 1) == 0 and rows % 16 == 0 and width % 128 == 0
    net = Network(size) if cube else None
    cut = net.first_cut() if cube else [[0]]
    plain_cut = [list(range(size))] if cube else [[0]]
    j_spans = split_by(local, (3, 3, 2)) if cube else split_even(local, 4)
    b_spans = [(2 * lo, 2 * hi) for lo, hi in split_by(local // 2, (3, 3, 2))]
    shifts = list(range(1, group))

    if cube:
        cols = [
            lax.dynamic_slice_in_dim(first_factor, lax.rem(me + shift, group) * width, width, 2)
            for shift in range(2)
        ]
        far = net.gather(cols[1])
        both = gather_plain(jnp.concatenate([second_factor, cols[0]], axis=2))
        second_whole = Whole(both.arrays, both.slots, False, (blk, 0))
        near = Whole(both.arrays, both.slots, False, (width, group))
        columns = [near, far]
    else:
        second_whole = gather_plain(second_factor)
        whole = gather_plain(first_factor).arrays[0]
        if whole.shape[0] > 1:
            whole = jnp.transpose(whole, (1, 0, 2, 3)).reshape(1, local, blk, blk)
        turned = jnp.roll(whole, -me * width, axis=3)
        near, far, turned = [
            Whole([array], [[0]], False) for array in (turned[..., :width], turned[..., width:], turned)
        ]
        columns = [turned]
    sends = expand(ids, tokens, far, shifts, j_spans, group, local)
    arrived = [
        [send(sends[(shift - 1) * len(j_spans) + at], shift, group) for shift in shifts]
        for at in range(len(j_spans))
    ]
    own = expand(ids, tokens, near, [0], [(0, local)], group, local)[0]

    held = {}
    backs = [(("back", place), b_span, (0, local)) for place, b_span in enumerate(b_spans)]
    for at, span in enumerate(j_spans):
        mix(
            ids, own, arrived[at], second_whole, tokens, upstream, held, span, group, local, cut, cube,
            ("term", (0, local)), backs,
        )
    returned = [[send(held[(key, shift)], shift, group) for shift in shifts] for key, _, _ in backs]
    parts = [held[("term", place)] for place in range(len(cut))]
    if cube:
        grad_second, marks = net.scatter(parts, scale, JOINED[0])
    else:
        grad_second, marks = scatter_plain(parts[0], rows, scale), []

    grad_tokens, sums, terms, chains = None, [], [], [marks]
    tie = lambda place: [array for chain, step in TIES.get(place, ()) if cube for array in chains[chain][step]]
    for place, b_span in enumerate(b_spans):
        grad_tokens, *parts = fold(
            ids, held["own"], [(array, b_span[0]) for array in returned[place]], tokens, upstream, columns,
            grad_tokens, b_span, group, local, cut, cube, tie(place),
        )
        if cube:
            total, marks = net.scatter(parts, scale, JOINED[1 + place])
            chains.append(marks)
            sums.append(total)
        else:
            terms.append(parts[0])
    if not cube:
        sums = [scatter_plain(jnp.concatenate(terms, axis=1), rows, scale)]
    return held["mixed"], grad_tokens, jnp.concatenate(sums), grad_second


def solution(mesh):
    placed = (P("dp", "mp"), P("dp", "mp"), P("mp", "dp", None), P("mp", "dp", None))
    return jax.shard_map(
        on_device, mesh=mesh, in_specs=placed, out_specs=placed, check_vma=False
    )
```

profile of v0, /device:TPU:0, one launch (start us, length us, event | category | flops | bytes accessed | tf_op | source)
XLA Modules:
  0.0 175.9 jit_solution(12618872633640194887)
XLA Ops:
  7.2 0.9 dynamic-slice_bitcast_fusion
  8.1 1.6 pad_maximum_fusion.2
  9.7 5.1 %collective-permute-start.2 = (bf16[1,16,16,128]{3,2,1,0:T(8,128)(2,1)S(1)}, bf16[1,16,16,128]{3,2,1,0:T(8,128)(2,1)S(1)}, u32[]{:S(2)}, u32[]{:S(2)}) collective-permute-start(bf16[1,16,16,128]{3,2,1,0:T(8,128)(2,1)S(1)} %get-tuple-element.73), channel_id=1, source_target_pairs={{0,24},{2,26},{4,28},{6,30},{8,16},{10,18},{12,20},{14,22},{16,8},... | collective-permute-start | bytes 196616 | tf_op jit(solution)/shard_map/ppermute | solution.py:123
  14.9 0.6 collective-permute-start
  15.5 1.9 %collective-permute-done.2 = bf16[1,16,16,128]{3,2,1,0:T(8,128)(2,1)S(1)} collective-permute-done((bf16[1,16,16,128]{3,2,1,0:T(8,128)(2,1)S(1)}, bf16[1,16,16,128]{3,2,1,0:T(8,128)(2,1)S(1)}, u32[]{:S(2)}, u32[]{:S(2)}) %collective-permute-start.2) | collective-permute-done | bytes 65568 | tf_op jit(solution)/shard_map/ppermute | solution.py:123
  17.4 3.0 %collective-permute-done.1 = bf16[1,16,16,128]{3,2,1,0:T(8,128)(2,1)S(1)} collective-permute-done((bf16[1,16,16,128]{3,2,1,0:T(8,128)(2,1)S(1)}, bf16[1,16,16,128]{3,2,1,0:T(8,128)(2,1)S(1)}, u32[]{:S(2)}, u32[]{:S(2)}) %collective-permute-start.1) | collective-permute-done | bytes 65568 | tf_op jit(solution)/shard_map/ppermute | solution.py:123
  20.5 1.6 collective-permute-start.3
  22.1 8.5 %collective-permute-done.3.refs_3_.refs_8_ = bf16[4,16,16,128]{3,2,1,0:T(8,128)(2,1)S(1)} collective-permute-done((bf16[4,16,16,128]{3,2,1,0:T(8,128)(2,1)S(1)}, bf16[4,16,16,128]{3,2,1,0:T(8,128)(2,1)S(1)}, u32[]{:S(2)}, u32[]{:S(2)}) %collective-permute-start.3) | collective-permute-done | bytes 262176 | tf_op jit(solution)/shard_map/ppermute | solution.py:123
  30.6 1.5 collective-permute-done.5.refs_5_.refs_10_
  32.1 7.9 %expand.3 = (bf16[6,128,512]{2,1,0:T(8,128)(2,1)}, bf16[6,128,512]{2,1,0:T(8,128)(2,1)}, bf16[4,128,512]{2,1,0:T(8,128)(2,1)}) custom-call(s32[2]{0:T(128)S(1)} %pad_add_fusion.ids_ref, bf16[512,4096]{1,0:T(8,128)(2,1)} %refs_3_.11, bf16[512,4096]{1,0:T(8,128)(2,1)} %refs_3_.11, bf16[4,16,16,128]{3,2,1,0:T(8,128)(2,1)S(1)} %pad_maximum_fusion.refs_2_.refs_7_, ...), custom_call_target="tpu_custom_call" | custom-call | flops 1 | bytes 1 | tf_op jit(solution)/shard_map/expand/pallas_call | solution.py:59
  40.0 1.7 collective-permute-start.8
  42.0 1.7 collective-permute-start.6
  43.7 16.4 %all-gather.3.cloned.1.call-done = bf16[256,16,384]{2,1,0:T(8,128)(2,1)} async-done(((bf16[16,16,384]{2,1,0:T(8,128)(2,1)}), bf16[256,16,384]{2,1,0:T(8,128)(2,1)}) %all-gather.3.cloned.1.call-update) | async-done | bytes 3145744 | tf_op jit(solution)/shard_map/all_gather | solution.py:424
  60.1 7.0 %expand.2.refs_0_ = bf16[16,128,512]{2,1,0:T(8,128)(2,1)S(1)} custom-call(s32[2]{0:T(128)S(1)} %pad_add_fusion.ids_ref, bf16[512,4096]{1,0:T(8,128)(2,1)} %refs_3_.11, bf16[512,4096]{1,0:T(8,128)(2,1)} %refs_3_.11, bf16[16,16,16,384]{3,2,1,0:T(8,128)(2,1)} %bitcast.13), custom_call_target="tpu_custom_call" | custom-call | flops 1 | bytes 1 | tf_op jit(solution)/shard_map/expand/pallas_call | solution.py:59
  67.1 8.7 %mix.3 = (bf16[512,4096]{1,0:T(8,128)(2,1)}, bf16[16,128,512]{2,1,0:T(8,128)(2,1)S(1)}, f32[8,16,16,256]{3,2,1,0:T(8,128)S(1)}, bf16[8,16,16,256]{3,2,1,0:T(8,12...) custom-call(s32[2]{0:T(128)S(1)} %pad_add_fusion.ids_ref, ...), custom_call_target="tpu_custom_call" | custom-call | flops 1 | bytes 1 | tf_op jit(solution)/shard_map/mix/pallas_call | solution.py:59
  75.9 1.6 collective-permute-done.7.refs_1_
  77.5 8.7 %mix.4 = (bf16[512,4096]{1,0:T(8,128)(2,1)}, bf16[16,128,512]{2,1,0:T(8,128)(2,1)S(1)}, f32[8,16,16,256]{3,2,1,0:T(8,128)S(1)}, bf16[8,16,16,256]{3,2,1,0:T(8,12...) custom-call(s32[2]{0:T(128)S(1)} %pad_add_fusion.ids_ref, ...), custom_call_target="tpu_custom_call", output_to_operand_aliasing={{0}: (8, {}), {1}: (9, {}), {2}: (10, {}), {3}: (11, {}), {... | custom-call | flops 1 | bytes 1 | tf_op jit(solution)/shard_map/mix/pallas_call | solution.py:59
  86.2 1.7 collective-permute-done.6.refs_1_
  87.9 6.6 %mix.5 = (bf16[512,4096]{1,0:T(8,128)(2,1)}, bf16[16,128,512]{2,1,0:T(8,128)(2,1)S(1)}, f32[8,16,16,256]{3,2,1,0:T(8,128)S(1)}, bf16[8,16,16,256]{3,2,1,0:T(8,12...) custom-call(s32[2]{0:T(128)S(1)} %pad_add_fusion.ids_ref, ...), custom_call_target="tpu_custom_call", output_to_operand_aliasing={{0}: (8, {}), {1}: (9, {}), {2}: (10, {}), {3}: (11, {}), {... | custom-call | flops 1 | bytes 1 | tf_op jit(solution)/shard_map/mix/pallas_call | solution.py:59
  94.5 1.7 collective-permute-start.11
  96.2 1.0 collective-permute-done.12
  97.3 1.7 collective-permute-start.13
  99.1 1.5 collective-permute-start.10
  100.6 10.8 %collective-permute-done.13 = bf16[4,16,16,256]{3,2,1,0:T(8,128)(2,1)S(1)} collective-permute-done((bf16[4,16,16,256]{3,2,1,0:T(8,128)(2,1)S(1)}, bf16[4,16,16,256]{3,2,1,0:T(8,128)(2,1)S(1)}, u32[]{:S(2)}, u32[]{:S(2)}) %collective-permute-start.13) | collective-permute-done | bytes 524320 | tf_op jit(solution)/shard_map/ppermute | solution.py:123
  111.5 3.3 %collective-permute-done.11.refs_1_ = bf16[16,48,512]{2,1,0:T(8,128)(2,1)S(1)} collective-permute-done((bf16[16,48,512]{2,1,0:T(8,128)(2,1)S(1)}, bf16[16,48,512]{2,1,0:T(8,128)(2,1)S(1)}, u32[]{:S(2)}, u32[]{:S(2)}) %collective-permute-start.11) | collective-permute-done | bytes 786464 | tf_op jit(solution)/shard_map/ppermute | solution.py:419
  114.8 5.1 %fold.3 = (bf16[512,4096]{1,0:T(8,128)(2,1)}, f32[8,6,16,256]{3,2,1,0:T(8,128)S(1)}, bf16[8,6,16,256]{3,2,1,0:T(8,128)(2,1)S(1)}) custom-call(s32[2]{0:T(128)S(1)} %pad_add_fusion.ids_ref, bf16[16,128,512]{2,1,0:T(8,128)(2,1)S(1)} %get-tuple-element.55.refs_0_, bf16[16,48,512]{2,1,0:T(8,128)(2,1)S(1)} %collective-permute-done.11.refs_1_, ...), custom_call_target="tpu_custom_call" | custom-call | flops 1 | bytes 1 | tf_op jit(solution)/shard_map/fold/pallas_call | solution.py:59
  119.9 1.7 collective-permute-start.9
  121.6 1.4 collective-permute-start.17
  123.1 2.9 %collective-permute-start.15 = (bf16[1,16,16,256]{3,2,1,0:T(8,128)(2,1)S(1)}, bf16[1,16,16,256]{3,2,1,0:T(8,128)(2,1)S(1)}, u32[]{:S(2)}, u32[]{:S(2)}) collective-permute-start(bf16[1,16,16,256]{3,2,1,0:T(8,128)(2,1)S(1)} %get-tuple-element.72.refs_11_), channel_id=1, source_target_pairs={{0,8},{2,10},{4,12},{6,14},{8,0},{10,2},{12,4},{14,6},{16,24},{18,... | collective-permute-start | bytes 393224 | tf_op jit(solution)/shard_map/ppermute | solution.py:123
  126.1 5.6 %collective-permute-done.10.refs_1_ = bf16[16,48,512]{2,1,0:T(8,128)(2,1)S(1)} collective-permute-done((bf16[16,48,512]{2,1,0:T(8,128)(2,1)S(1)}, bf16[16,48,512]{2,1,0:T(8,128)(2,1)S(1)}, u32[]{:S(2)}, u32[]{:S(2)}) %collective-permute-start.10) | collective-permute-done | bytes 786464 | tf_op jit(solution)/shard_map/ppermute | solution.py:419
  131.7 1.7 collective-permute-start.18
  133.4 5.1 %fold.4 = (bf16[512,4096]{1,0:T(8,128)(2,1)}, f32[8,6,16,256]{3,2,1,0:T(8,128)S(1)}, bf16[8,6,16,256]{3,2,1,0:T(8,128)(2,1)S(1)}) custom-call(s32[2]{0:T(128)S(1)} %pad_add_fusion.ids_ref, bf16[16,128,512]{2,1,0:T(8,128)(2,1)S(1)} %get-tuple-element.55.refs_0_, ...), custom_call_target="tpu_custom_call", output_to_operand_aliasing={{0}: (12, {})} | custom-call | flops 1 | bytes 1 | tf_op jit(solution)/shard_map/fold/pallas_call | solution.py:59
  138.8 1.4 collective-permute-done.20
  140.3 0.4 collective-permute-start.21
  140.7 3.3 %collective-permute-done.19 = bf16[2,6,16,256]{3,2,1,0:T(8,128)(2,1)S(1)} collective-permute-done((bf16[2,6,16,256]{3,2,1,0:T(8,128)(2,1)S(1)}, bf16[2,6,16,256]{3,2,1,0:T(8,128)(2,1)S(1)}, u32[]{:S(2)}, u32[]{:S(2)}) %collective-permute-start.19) | collective-permute-done | bytes 98336 | tf_op jit(solution)/shard_map/ppermute | solution.py:123
  144.0 3.3 %collective-permute-done.21 = bf16[4,6,16,256]{3,2,1,0:T(8,128)(2,1)S(1)} collective-permute-done((bf16[4,6,16,256]{3,2,1,0:T(8,128)(2,1)S(1)}, bf16[4,6,16,256]{3,2,1,0:T(8,128)(2,1)S(1)}, u32[]{:S(2)}, u32[]{:S(2)}) %collective-permute-start.21) | collective-permute-done | bytes 196640 | tf_op jit(solution)/shard_map/ppermute | solution.py:123
  147.3 3.9 %fold.5 = (bf16[512,4096]{1,0:T(8,128)(2,1)}, f32[8,4,16,256]{3,2,1,0:T(8,128)S(1)}, bf16[8,4,16,256]{3,2,1,0:T(8,128)(2,1)S(1)}) custom-call(s32[2]{0:T(128)S(1)} %pad_add_fusion.ids_ref, bf16[16,128,512]{2,1,0:T(8,128)(2,1)S(1)} %get-tuple-element.55.refs_0_, ...), custom_call_target="tpu_custom_call", output_to_operand_aliasing={{0}: (12, {})} | custom-call | flops 1 | bytes 1 | tf_op jit(solution)/shard_map/fold/pallas_call | solution.py:59
  151.2 0.7 collective-permute-start.22
  151.9 0.8 collective-permute-done.25
  152.8 0.4 collective-permute-start.26
  153.2 4.1 %collective-permute-done.22 = bf16[1,6,16,256]{3,2,1,0:T(8,128)(2,1)S(1)} collective-permute-done((bf16[1,6,16,256]{3,2,1,0:T(8,128)(2,1)S(1)}, bf16[1,6,16,256]{3,2,1,0:T(8,128)(2,1)S(1)}, u32[]{:S(2)}, u32[]{:S(2)}) %collective-permute-start.22) | collective-permute-done | bytes 49184 | tf_op jit(solution)/shard_map/ppermute | solution.py:123
  157.4 1.0 collective-permute-done.26
  158.4 1.1 collective-permute-start.27
  159.6 3.2 %collective-permute-done.23 = bf16[2,6,16,256]{3,2,1,0:T(8,128)(2,1)S(1)} collective-permute-done((bf16[2,6,16,256]{3,2,1,0:T(8,128)(2,1)S(1)}, bf16[2,6,16,256]{3,2,1,0:T(8,128)(2,1)S(1)}, u32[]{:S(2)}, u32[]{:S(2)}) %collective-permute-start.23) | collective-permute-done | bytes 98336 | tf_op jit(solution)/shard_map/ppermute | solution.py:123
  162.9 0.6 collective-permute-done.27
  163.5 2.4 %collective-permute-start.28 = (bf16[1,4,16,256]{3,2,1,0:T(8,128)(2,1)S(1)}, bf16[1,4,16,256]{3,2,1,0:T(8,128)(2,1)S(1)}, u32[]{:S(2)}, u32[]{:S(2)}) collective-permute-start(bf16[1,4,16,256]{3,2,1,0:T(8,128)(2,1)S(1)} %add_convert_fusion.12), channel_id=1, source_target_pairs={{0,16},{2,18},{4,20},{6,22},{8,24},{10,26},{12,28},{14,30},{16,0},... | collective-permute-start | bytes 98312 | tf_op jit(solution)/shard_map/ppermute | solution.py:123
  165.9 2.1 %collective-permute-done.24 = bf16[1,6,16,256]{3,2,1,0:T(8,128)(2,1)S(1)} collective-permute-done((bf16[1,6,16,256]{3,2,1,0:T(8,128)(2,1)S(1)}, bf16[1,6,16,256]{3,2,1,0:T(8,128)(2,1)S(1)}, u32[]{:S(2)}, u32[]{:S(2)}) %collective-permute-start.24) | collective-permute-done | bytes 49184 | tf_op jit(solution)/shard_map/ppermute | solution.py:123
  168.4 0.7 pad_maximum_fusion.1
  (43 shorter events, 2.0 us)
Async XLA Ops:
  7.2 52.9 %all-gather.3.cloned.1.call-start = ((), (), s32[]{:S(2)}) async-start(), calls=%async_computation | async-start | bytes 3342336 | tf_op jit(solution)/shard_map/all_gather | solution.py:424
  9.7 7.7 %collective-permute-start.2 = (bf16[1,16,16,128]{3,2,1,0:T(8,128)(2,1)S(1)}, bf16[1,16,16,128]{3,2,1,0:T(8,128)(2,1)S(1)}, u32[]{:S(2)}, u32[]{:S(2)}) collective-permute-start(bf16[1,16,16,128]{3,2,1,0:T(8,128)(2,1)S(1)} %get-tuple-element.73), channel_id=1, source_target_pairs={{0,24},{2,26},{4,28},{6,30},{8,16},{10,18},{12,20},{14,22},{16,8},... | collective-permute-start | bytes 196616 | tf_op jit(solution)/shard_map/ppermute | solution.py:123
  14.9 5.6 %collective-permute-start.1 = (bf16[1,16,16,128]{3,2,1,0:T(8,128)(2,1)S(1)}, bf16[1,16,16,128]{3,2,1,0:T(8,128)(2,1)S(1)}, u32[]{:S(2)}, u32[]{:S(2)}) collective-permute-start(bf16[1,16,16,128]{3,2,1,0:T(8,128)(2,1)S(1)} %get-tuple-element.73), channel_id=1, source_target_pairs={{0,16},{2,18},{4,20},{6,22},{8,24},{10,26},{12,28},{14,30},{16,0},... | collective-permute-start | bytes 196616 | tf_op jit(solution)/shard_map/ppermute | solution.py:123
  14.9 5.6 %collective-permute-start = (bf16[1,16,16,128]{3,2,1,0:T(8,128)(2,1)S(1)}, bf16[1,16,16,128]{3,2,1,0:T(8,128)(2,1)S(1)}, u32[]{:S(2)}, u32[]{:S(2)}) collective-permute-start(bf16[1,16,16,128]{3,2,1,0:T(8,128)(2,1)S(1)} %get-tuple-element.73), channel_id=1, source_target_pairs={{0,8},{2,10},{4,12},{6,14},{8,0},{10,2},{12,4},{14,6},{16,24},{18,... | collective-permute-start | bytes 196616 | tf_op jit(solution)/shard_map/ppermute | solution.py:123
  20.5 10.0 %collective-permute-start.3 = (bf16[4,16,16,128]{3,2,1,0:T(8,128)(2,1)S(1)}, bf16[4,16,16,128]{3,2,1,0:T(8,128)(2,1)S(1)}, u32[]{:S(2)}, u32[]{:S(2)}) collective-permute-start(bf16[4,16,16,128]{3,2,1,0:T(8,128)(2,1)S(1)} %pad_maximum_fusion.refs_2_.refs_7_), channel_id=1, source_target_pairs={{0,4},{2,6},{4,0},{6,2},{8,12},{10,14},{12,8},{14,10},{16,20},{18,... | collective-permute-start | bytes 786440 | tf_op jit(solution)/shard_map/ppermute | solution.py:123
  22.1 8.6 %collective-permute-start.4 = (bf16[4,16,16,128]{3,2,1,0:T(8,128)(2,1)S(1)}, bf16[4,16,16,128]{3,2,1,0:T(8,128)(2,1)S(1)}, u32[]{:S(2)}, u32[]{:S(2)}) collective-permute-start(bf16[4,16,16,128]{3,2,1,0:T(8,128)(2,1)S(1)} %pad_maximum_fusion.refs_2_.refs_7_), channel_id=1, source_target_pairs={{0,2},{2,0},{4,6},{6,4},{8,10},{10,8},{12,14},{14,12},{16,18},{18,... | collective-permute-start | bytes 786440 | tf_op jit(solution)/shard_map/ppermute | solution.py:123
  30.6 1.5 collective-permute-start.5
  40.0 27.1 %collective-permute-start.8 = (bf16[6,128,512]{2,1,0:T(8,128)(2,1)}, bf16[6,128,512]{2,1,0:T(8,128)(2,1)S(1)}, u32[]{:S(2)}, u32[]{:S(2)}) collective-permute-start(bf16[6,128,512]{2,1,0:T(8,128)(2,1)} %get-tuple-element.39), channel_id=1, source_target_pairs={{0,1},{1,0},{2,3},{3,2},{4,5},{5,4},{6,7},{7,6},{8,9},{9,8},{10,11... | collective-permute-start | bytes 2359304 | tf_op jit(solution)/shard_map/ppermute | solution.py:419
  41.7 35.8 %collective-permute-start.7 = (bf16[6,128,512]{2,1,0:T(8,128)(2,1)}, bf16[6,128,512]{2,1,0:T(8,128)(2,1)S(1)}, u32[]{:S(2)}, u32[]{:S(2)}) collective-permute-start(bf16[6,128,512]{2,1,0:T(8,128)(2,1)} %get-tuple-element.38), channel_id=1, source_target_pairs={{0,1},{1,0},{2,3},{3,2},{4,5},{5,4},{6,7},{7,6},{8,9},{9,8},{10,11... | collective-permute-start | bytes 2359304 | tf_op jit(solution)/shard_map/ppermute | solution.py:419
  42.0 45.9 %collective-permute-start.6 = (bf16[4,128,512]{2,1,0:T(8,128)(2,1)}, bf16[4,128,512]{2,1,0:T(8,128)(2,1)S(1)}, u32[]{:S(2)}, u32[]{:S(2)}) collective-permute-start(bf16[4,128,512]{2,1,0:T(8,128)(2,1)} %get-tuple-element.37), channel_id=1, source_target_pairs={{0,1},{1,0},{2,3},{3,2},{4,5},{5,4},{6,7},{7,6},{8,9},{9,8},{10,11... | collective-permute-start | bytes 1572872 | tf_op jit(solution)/shard_map/ppermute | solution.py:419
  94.5 2.7 %collective-permute-start.12 = (bf16[8,16,16,256]{3,2,1,0:T(8,128)(2,1)S(1)}, bf16[8,16,16,256]{3,2,1,0:T(8,128)(2,1)S(1)}, u32[]{:S(2)}, u32[]{:S(2)}) collective-permute-start(bf16[8,16,16,256]{3,2,1,0:T(8,128)(2,1)S(1)} %get-tuple-element.60), channel_id=1, source_target_pairs={{0,2},{2,0},{4,6},{6,4},{8,10},{10,8},{12,14},{14,12},{16,18},{18,... | collective-permute-start | bytes 3145736 | tf_op jit(solution)/shard_map/ppermute | solution.py:123
  94.5 20.3 %collective-permute-start.11 = (bf16[16,48,512]{2,1,0:T(8,128)(2,1)S(1)}, bf16[16,48,512]{2,1,0:T(8,128)(2,1)S(1)}, u32[]{:S(2)}, u32[]{:S(2)}) collective-permute-start(bf16[16,48,512]{2,1,0:T(8,128)(2,1)S(1)} %get-tuple-element.58), channel_id=1, source_target_pairs={{0,1},{1,0},{2,3},{3,2},{4,5},{5,4},{6,7},{7,6},{8,9},{9,8},{10,11... | collective-permute-start | bytes 2359304 | tf_op jit(solution)/shard_map/ppermute | solution.py:419
  97.3 14.0 %collective-permute-start.13 = (bf16[4,16,16,256]{3,2,1,0:T(8,128)(2,1)S(1)}, bf16[4,16,16,256]{3,2,1,0:T(8,128)(2,1)S(1)}, u32[]{:S(2)}, u32[]{:S(2)}) collective-permute-start(bf16[4,16,16,256]{3,2,1,0:T(8,128)(2,1)S(1)} %add_convert_fusion), channel_id=1, source_target_pairs={{0,4},{2,6},{4,0},{6,2},{8,12},{10,14},{12,8},{14,10},{16,20},{18,... | collective-permute-start | bytes 1572872 | tf_op jit(solution)/shard_map/ppermute | solution.py:123
  99.1 32.6 %collective-permute-start.10 = (bf16[16,48,512]{2,1,0:T(8,128)(2,1)S(1)}, bf16[16,48,512]{2,1,0:T(8,128)(2,1)S(1)}, u32[]{:S(2)}, u32[]{:S(2)}) collective-permute-start(bf16[16,48,512]{2,1,0:T(8,128)(2,1)S(1)} %get-tuple-element.57), channel_id=1, source_target_pairs={{0,1},{1,0},{2,3},{3,2},{4,5},{5,4},{6,7},{7,6},{8,9},{9,8},{10,11... | collective-permute-start | bytes 2359304 | tf_op jit(solution)/shard_map/ppermute | solution.py:419
  119.9 3.1 %collective-permute-start.14 = (bf16[8,6,16,256]{3,2,1,0:T(8,128)(2,1)S(1)}, bf16[8,6,16,256]{3,2,1,0:T(8,128)(2,1)S(1)}, u32[]{:S(2)}, u32[]{:S(2)}) collective-permute-start(bf16[8,6,16,256]{3,2,1,0:T(8,128)(2,1)S(1)} %get-tuple-element.63), channel_id=1, source_target_pairs={{0,2},{2,0},{4,6},{6,4},{8,10},{10,8},{12,14},{14,12},{16,18},{18,... | collective-permute-start | bytes 1179656 | tf_op jit(solution)/shard_map/ppermute | solution.py:123
  119.9 27.4 %collective-permute-start.9 = (bf16[16,32,512]{2,1,0:T(8,128)(2,1)S(1)}, bf16[16,32,512]{2,1,0:T(8,128)(2,1)S(1)}, u32[]{:S(2)}, u32[]{:S(2)}) collective-permute-start(bf16[16,32,512]{2,1,0:T(8,128)(2,1)S(1)} %get-tuple-element.56), channel_id=1, source_target_pairs={{0,1},{1,0},{2,3},{3,2},{4,5},{5,4},{6,7},{7,6},{8,9},{9,8},{10,11... | collective-permute-start | bytes 1572872 | tf_op jit(solution)/shard_map/ppermute | solution.py:419
  121.6 16.9 %collective-permute-start.17 = (bf16[1,16,16,256]{3,2,1,0:T(8,128)(2,1)S(1)}, bf16[1,16,16,256]{3,2,1,0:T(8,128)(2,1)S(1)}, u32[]{:S(2)}, u32[]{:S(2)}) collective-permute-start(bf16[1,16,16,256]{3,2,1,0:T(8,128)(2,1)S(1)} %get-tuple-element.70.refs_13_), channel_id=1, source_target_pairs={{0,24},{2,26},{4,28},{6,30},{8,16},{10,18},{12,20},{14,22},{16,8},... | collective-permute-start | bytes 393224 | tf_op jit(solution)/shard_map/ppermute | solution.py:123
  123.1 15.4 %collective-permute-start.16 = (bf16[1,16,16,256]{3,2,1,0:T(8,128)(2,1)S(1)}, bf16[1,16,16,256]{3,2,1,0:T(8,128)(2,1)S(1)}, u32[]{:S(2)}, u32[]{:S(2)}) collective-permute-start(bf16[1,16,16,256]{3,2,1,0:T(8,128)(2,1)S(1)} %get-tuple-element.71.refs_12_), channel_id=1, source_target_pairs={{0,16},{2,18},{4,20},{6,22},{8,24},{10,26},{12,28},{14,30},{16,0},... | collective-permute-start | bytes 393224 | tf_op jit(solution)/shard_map/ppermute | solution.py:123
  123.1 15.4 %collective-permute-start.15 = (bf16[1,16,16,256]{3,2,1,0:T(8,128)(2,1)S(1)}, bf16[1,16,16,256]{3,2,1,0:T(8,128)(2,1)S(1)}, u32[]{:S(2)}, u32[]{:S(2)}) collective-permute-start(bf16[1,16,16,256]{3,2,1,0:T(8,128)(2,1)S(1)} %get-tuple-element.72.refs_11_), channel_id=1, source_target_pairs={{0,8},{2,10},{4,12},{6,14},{8,0},{10,2},{12,4},{14,6},{16,24},{18,... | collective-permute-start | bytes 393224 | tf_op jit(solution)/shard_map/ppermute | solution.py:123
  131.7 7.0 %collective-permute-start.18 = (bf16[4,6,16,256]{3,2,1,0:T(8,128)(2,1)S(1)}, bf16[4,6,16,256]{3,2,1,0:T(8,128)(2,1)S(1)}, u32[]{:S(2)}, u32[]{:S(2)}) collective-permute-start(bf16[4,6,16,256]{3,2,1,0:T(8,128)(2,1)S(1)} %add_convert_fusion.2.refs_12_), channel_id=1, source_target_pairs={{0,4},{2,6},{4,0},{6,2},{8,12},{10,14},{12,8},{14,10},{16,20},{18,... | collective-permute-start | bytes 589832 | tf_op jit(solution)/shard_map/ppermute | solution.py:123
  138.5 1.7 collective-permute-start.20
  138.6 12.6 %copy-start = (f32[16,16,256]{2,1,0:T(8,128)}, f32[16,16,256]{2,1,0:T(8,128)S(1)}, u32[]{:S(2)}) copy-start(f32[16,16,256]{2,1,0:T(8,128)S(1)} %multiply_bitcast_fusion.refs_12_) | copy-start | bytes 786436
  138.7 5.2 %collective-permute-start.19 = (bf16[2,6,16,256]{3,2,1,0:T(8,128)(2,1)S(1)}, bf16[2,6,16,256]{3,2,1,0:T(8,128)(2,1)S(1)}, u32[]{:S(2)}, u32[]{:S(2)}) collective-permute-start(bf16[2,6,16,256]{3,2,1,0:T(8,128)(2,1)S(1)} %add_convert_fusion.8), channel_id=1, source_target_pairs={{0,8},{2,10},{4,12},{6,14},{8,0},{10,2},{12,4},{14,6},{16,24},{18,... | collective-permute-start | bytes 294920 | tf_op jit(solution)/shard_map/ppermute | solution.py:123
  140.3 7.0 %collective-permute-start.21 = (bf16[4,6,16,256]{3,2,1,0:T(8,128)(2,1)S(1)}, bf16[4,6,16,256]{3,2,1,0:T(8,128)(2,1)S(1)}, u32[]{:S(2)}, u32[]{:S(2)}) collective-permute-start(bf16[4,6,16,256]{3,2,1,0:T(8,128)(2,1)S(1)} %add_convert_fusion.1), channel_id=1, source_target_pairs={{0,4},{2,6},{4,0},{6,2},{8,12},{10,14},{12,8},{14,10},{16,20},{18,... | collective-permute-start | bytes 589832 | tf_op jit(solution)/shard_map/ppermute | solution.py:123
  151.2 1.5 collective-permute-start.25
  151.2 6.1 %collective-permute-start.22 = (bf16[1,6,16,256]{3,2,1,0:T(8,128)(2,1)S(1)}, bf16[1,6,16,256]{3,2,1,0:T(8,128)(2,1)S(1)}, u32[]{:S(2)}, u32[]{:S(2)}) collective-permute-start(bf16[1,6,16,256]{3,2,1,0:T(8,128)(2,1)S(1)} %add_convert_fusion.11.refs_13_), channel_id=1, source_target_pairs={{0,16},{2,18},{4,20},{6,22},{8,24},{10,26},{12,28},{14,30},{16,0},... | collective-permute-start | bytes 147464 | tf_op jit(solution)/shard_map/ppermute | solution.py:123
  152.8 5.6 %collective-permute-start.26 = (bf16[4,4,16,256]{3,2,1,0:T(8,128)(2,1)S(1)}, bf16[4,4,16,256]{3,2,1,0:T(8,128)(2,1)S(1)}, u32[]{:S(2)}, u32[]{:S(2)}) collective-permute-start(bf16[4,4,16,256]{3,2,1,0:T(8,128)(2,1)S(1)} %add_convert_fusion.3), channel_id=1, source_target_pairs={{0,4},{2,6},{4,0},{6,2},{8,12},{10,14},{12,8},{14,10},{16,20},{18,... | collective-permute-start | bytes 393224 | tf_op jit(solution)/shard_map/ppermute | solution.py:123
  157.4 5.4 %collective-permute-start.23 = (bf16[2,6,16,256]{3,2,1,0:T(8,128)(2,1)S(1)}, bf16[2,6,16,256]{3,2,1,0:T(8,128)(2,1)S(1)}, u32[]{:S(2)}, u32[]{:S(2)}) collective-permute-start(bf16[2,6,16,256]{3,2,1,0:T(8,128)(2,1)S(1)} %add_convert_fusion.7.refs_14_), channel_id=1, source_target_pairs={{0,8},{2,10},{4,12},{6,14},{8,0},{10,2},{12,4},{14,6},{16,24},{18,... | collective-permute-start | bytes 294920 | tf_op jit(solution)/shard_map/ppermute | solution.py:123
  158.4 5.0 %collective-permute-start.27 = (bf16[2,4,16,256]{3,2,1,0:T(8,128)(2,1)S(1)}, bf16[2,4,16,256]{3,2,1,0:T(8,128)(2,1)S(1)}, u32[]{:S(2)}, u32[]{:S(2)}) collective-permute-start(bf16[2,4,16,256]{3,2,1,0:T(8,128)(2,1)S(1)} %add_convert_fusion.9), channel_id=1, source_target_pairs={{0,8},{2,10},{4,12},{6,14},{8,0},{10,2},{12,4},{14,6},{16,24},{18,... | collective-permute-start | bytes 196616 | tf_op jit(solution)/shard_map/ppermute | solution.py:123
  162.8 5.2 %collective-permute-start.24 = (bf16[1,6,16,256]{3,2,1,0:T(8,128)(2,1)S(1)}, bf16[1,6,16,256]{3,2,1,0:T(8,128)(2,1)S(1)}, u32[]{:S(2)}, u32[]{:S(2)}) collective-permute-start(bf16[1,6,16,256]{3,2,1,0:T(8,128)(2,1)S(1)} %add_convert_fusion.10), channel_id=1, source_target_pairs={{0,16},{2,18},{4,20},{6,22},{8,24},{10,26},{12,28},{14,30},{16,0},... | collective-permute-start | bytes 147464 | tf_op jit(solution)/shard_map/ppermute | solution.py:123
  163.5 4.9 %collective-permute-start.28 = (bf16[1,4,16,256]{3,2,1,0:T(8,128)(2,1)S(1)}, bf16[1,4,16,256]{3,2,1,0:T(8,128)(2,1)S(1)}, u32[]{:S(2)}, u32[]{:S(2)}) collective-permute-start(bf16[1,4,16,256]{3,2,1,0:T(8,128)(2,1)S(1)} %add_convert_fusion.12), channel_id=1, source_target_pairs={{0,16},{2,18},{4,20},{6,22},{8,24},{10,26},{12,28},{14,30},{16,0},... | collective-permute-start | bytes 98312 | tf_op jit(solution)/shard_map/ppermute | solution.py:123
Sparse Core Ops, SparseCore 0:
  10.9 49.2 all-gather.2
where the time goes:
time: 177 us; the launch traced here: 176 us
  waiting for transfers between devices  75.4 us (43%)
  Pallas kernels  53.1 us (30%)
  starting transfers between devices  29.1 us (16%)
  between operations  14.2 us (8%)
  other arithmetic  3.33 us (2%)
    pallas_call x8, Pallas kernels, call(): pl.pallas_call(body, grid_spec=pltpu.PrefetchScalarGridSpec(num_scalar_pr...  53.1 us
    ppermute x23, waiting for transfers between devices, swap(): lax.ppermute(array, 'dp', [(at, at ^ mask) for at in range(self.size)])  46.8 us
    ppermute x23, starting transfers between devices, swap(): lax.ppermute(array, 'dp', [(at, at ^ mask) for at in range(self.size)])  20.5 us
    all_gather x1, waiting for transfers between devices, gather_plain(): whole = lax.all_gather(shard, 'dp', axis=0, tiled=False)  16.4 us
    ppermute x6, waiting for transfers between devices, send(): lax.ppermute(array, 'mp', [(at, (at + shift) % group) for at in range(gro...  12.2 us
    ppermute x6, starting transfers between devices, send(): lax.ppermute(array, 'mp', [(at, (at + shift) % group) for at in range(gro...  8.56 us
  transfers between devices with their start and end apart: 30, of which 21 were waited for; matrix products, arithmetic and copies ran while one was open for 1% of the time, Pallas kernels for 24%

commit v1 on v0

--- a/solution.py
+++ b/solution.py
@@ -12,6 +12,7 @@
 F32 = jnp.float32
 ROOT_HALF = math.sqrt(0.5)
 DENSITY = 1.0 / math.sqrt(2.0 * math.pi)
+TOGETHER = 2
 JOINED = (True, False, False, False)
 TIES = {0: ((0, 2),), 1: ((1, 1),), 2: ((0, 3), (1, 3), (2, 2))}
 VMEM = 20 * 1024 * 1024
@@ -137,12 +138,14 @@
     def first_cut(self):
         return self.cut(self.order, self.rounds[0])
 
-    def scatter(self, parts, scale, joined=False):
+    def scatter(self, parts, scale, joined=False, closed=True):
         rounds = self.rounds[: len(self.near)] + [tuple(self.far)] if joined else self.rounds
         slots = self.first_cut()[0]
         terms, sends, marks = [parts[0]], parts[1:], []
         for step, bits in enumerate(rounds):
             marks.append(sends)
+            if step + 1 == len(rounds) and not closed:
+                return (terms, sends[0]), marks
             terms += [self.swap(piece, mask) for piece, mask in zip(sends, combos(bits)[1:])]
             if step + 1 < len(rounds):
                 lists = self.cut(slots, rounds[step + 1])
@@ -152,6 +155,15 @@
                 slots = lists[0]
         result = sum(term[0].astype(F32) for term in terms) * scale
         return result, marks + [[result]]
+
+    def close(self, opened, scale):
+        got = self.swap(jnp.concatenate([sent for _, sent in opened], axis=1), self.rounds[-1][0])
+        results, start = [], 0
+        for terms, sent in opened:
+            part = got[:, start : start + sent.shape[1]]
+            results.append(sum(term[0].astype(F32) for term in terms + [part]) * scale)
+            start += sent.shape[1]
+        return results
 
 
 def tiles(array, rows, cols, down, along, at):
@@ -490,7 +502,7 @@
     else:
         grad_second, marks = scatter_plain(parts[0], rows, scale), []
 
-    grad_tokens, sums, terms, chains = None, [], [], [marks]
+    grad_tokens, sums, terms, opened, chains = None, [], [], [], [marks]
     tie = lambda place: [array for chain, step in TIES.get(place, ()) if cube for array in chains[chain][step]]
     for place, b_span in enumerate(b_spans):
         grad_tokens, *parts = fold(
@@ -498,9 +510,14 @@
             grad_tokens, b_span, group, local, cut, cube, tie(place),
         )
         if cube:
-            total, marks = net.scatter(parts, scale, JOINED[1 + place])
+            total, marks = net.scatter(parts, scale, JOINED[1 + place], place >= TOGETHER)
             chains.append(marks)
-            sums.append(total)
+            if place >= TOGETHER:
+                sums.append(total)
+            else:
+                opened.append(total)
+                if len(opened) == TOGETHER:
+                    sums += net.close(opened, scale)
         else:
             terms.append(parts[0])
     if not cube:

time: 177 us -> 177 us (level)
    ppermute x23 -> x22, waiting for transfers between devices: 46.8 us -> 48.3 us  [swap(): lax.ppermute(array, 'dp', [(at, at ^ mask) for at in range(self.size)])]
    ppermute x23 -> x22, starting transfers between devices: 20.5 us -> 19.2 us  [swap(): lax.ppermute(array, 'dp', [(at, at ^ mask) for at in range(self.size)])]
  transfers between devices with their start and end apart: 30 -> 29, of which waited for: 21 -> 20; matrix products, arithmetic and copies ran while one was open for 1% -> 1% of each run, Pallas kernels for 24% -> 24%
where the time goes in v1:
time: 177 us; the launch traced here: 176 us
  waiting for transfers between devices  76.9 us (43%)
  Pallas kernels  53.1 us (30%)
  starting transfers between devices  27.8 us (16%)
  between operations  14.2 us (8%)
  other arithmetic  3.33 us (2%)
    pallas_call x8, Pallas kernels, call(): pl.pallas_call(body, grid_spec=pltpu.PrefetchScalarGridSpec(num_scalar_pr...  53.1 us
    ppermute x22, waiting for transfers between devices, swap(): lax.ppermute(array, 'dp', [(at, at ^ mask) for at in range(self.size)])  48.3 us
    ppermute x22, starting transfers between devices, swap(): lax.ppermute(array, 'dp', [(at, at ^ mask) for at in range(self.size)])  19.2 us
    all_gather x1, waiting for transfers between devices, gather_plain(): whole = lax.all_gather(shard, 'dp', axis=0, tiled=False)  16.4 us
    ppermute x6, waiting for transfers between devices, send(): lax.ppermute(array, 'mp', [(at, (at + shift) % group) for at in range(gro...  12.2 us
    ppermute x6, starting transfers between devices, send(): lax.ppermute(array, 'mp', [(at, (at + shift) % group) for at in range(gro...  8.56 us
  transfers between devices with their start and end apart: 29, of which 20 were waited for; matrix products, arithmetic and copies ran while one was open for 1% of the time, Pallas kernels for 24%

profile of v1, /device:TPU:0, one launch (start us, length us, event | category | flops | bytes accessed | tf_op | source)
XLA Modules:
  0.0 176.2 jit_solution(1685281848054745806)
XLA Ops:
  7.2 0.9 dynamic-slice_bitcast_fusion
  8.1 1.6 pad_maximum_fusion.2
  9.7 5.1 %collective-permute-start.2 = (bf16[1,16,16,128]{3,2,1,0:T(8,128)(2,1)S(1)}, bf16[1,16,16,128]{3,2,1,0:T(8,128)(2,1)S(1)}, u32[]{:S(2)}, u32[]{:S(2)}) collective-permute-start(bf16[1,16,16,128]{3,2,1,0:T(8,128)(2,1)S(1)} %get-tuple-element.73), channel_id=1, source_target_pairs={{0,24},{2,26},{4,28},{6,30},{8,16},{10,18},{12,20},{14,22},{16,8},... | collective-permute-start | bytes 196616 | tf_op jit(solution)/shard_map/ppermute | solution.py:124
  14.9 0.6 collective-permute-start
  15.5 1.9 %collective-permute-done.2 = bf16[1,16,16,128]{3,2,1,0:T(8,128)(2,1)S(1)} collective-permute-done((bf16[1,16,16,128]{3,2,1,0:T(8,128)(2,1)S(1)}, bf16[1,16,16,128]{3,2,1,0:T(8,128)(2,1)S(1)}, u32[]{:S(2)}, u32[]{:S(2)}) %collective-permute-start.2) | collective-permute-done | bytes 65568 | tf_op jit(solution)/shard_map/ppermute | solution.py:124
  17.4 3.0 %collective-permute-done.1 = bf16[1,16,16,128]{3,2,1,0:T(8,128)(2,1)S(1)} collective-permute-done((bf16[1,16,16,128]{3,2,1,0:T(8,128)(2,1)S(1)}, bf16[1,16,16,128]{3,2,1,0:T(8,128)(2,1)S(1)}, u32[]{:S(2)}, u32[]{:S(2)}) %collective-permute-start.1) | collective-permute-done | bytes 65568 | tf_op jit(solution)/shard_map/ppermute | solution.py:124
  20.5 1.6 collective-permute-start.3
  22.1 8.5 %collective-permute-done.3.refs_3_.refs_8_ = bf16[4,16,16,128]{3,2,1,0:T(8,128)(2,1)S(1)} collective-permute-done((bf16[4,16,16,128]{3,2,1,0:T(8,128)(2,1)S(1)}, bf16[4,16,16,128]{3,2,1,0:T(8,128)(2,1)S(1)}, u32[]{:S(2)}, u32[]{:S(2)}) %collective-permute-start.3) | collective-permute-done | bytes 262176 | tf_op jit(solution)/shard_map/ppermute | solution.py:124
  30.6 1.5 collective-permute-done.5.refs_5_.refs_10_
  32.1 7.9 %expand.3 = (bf16[6,128,512]{2,1,0:T(8,128)(2,1)}, bf16[6,128,512]{2,1,0:T(8,128)(2,1)}, bf16[4,128,512]{2,1,0:T(8,128)(2,1)}) custom-call(s32[2]{0:T(128)S(1)} %pad_add_fusion.ids_ref, bf16[512,4096]{1,0:T(8,128)(2,1)} %refs_3_.11, bf16[512,4096]{1,0:T(8,128)(2,1)} %refs_3_.11, bf16[4,16,16,128]{3,2,1,0:T(8,128)(2,1)S(1)} %pad_maximum_fusion.refs_2_.refs_7_, ...), custom_call_target="tpu_custom_call" | custom-call | flops 1 | bytes 1 | tf_op jit(solution)/shard_map/expand/pallas_call | solution.py:60
  40.0 1.7 collective-permute-start.8
  42.0 1.7 collective-permute-start.6
  43.7 16.4 %all-gather.3.cloned.1.call-done = bf16[256,16,384]{2,1,0:T(8,128)(2,1)} async-done(((bf16[16,16,384]{2,1,0:T(8,128)(2,1)}), bf16[256,16,384]{2,1,0:T(8,128)(2,1)}) %all-gather.3.cloned.1.call-update) | async-done | bytes 3145744 | tf_op jit(solution)/shard_map/all_gather | solution.py:436
  60.1 7.0 %expand.2.refs_0_ = bf16[16,128,512]{2,1,0:T(8,128)(2,1)S(1)} custom-call(s32[2]{0:T(128)S(1)} %pad_add_fusion.ids_ref, bf16[512,4096]{1,0:T(8,128)(2,1)} %refs_3_.11, bf16[512,4096]{1,0:T(8,128)(2,1)} %refs_3_.11, bf16[16,16,16,384]{3,2,1,0:T(8,128)(2,1)} %bitcast.13), custom_call_target="tpu_custom_call" | custom-call | flops 1 | bytes 1 | tf_op jit(solution)/shard_map/expand/pallas_call | solution.py:60
  67.1 8.7 %mix.3 = (bf16[512,4096]{1,0:T(8,128)(2,1)}, bf16[16,128,512]{2,1,0:T(8,128)(2,1)S(1)}, f32[8,16,16,256]{3,2,1,0:T(8,128)S(1)}, bf16[8,16,16,256]{3,2,1,0:T(8,12...) custom-call(s32[2]{0:T(128)S(1)} %pad_add_fusion.ids_ref, ...), custom_call_target="tpu_custom_call" | custom-call | flops 1 | bytes 1 | tf_op jit(solution)/shard_map/mix/pallas_call | solution.py:60
  75.9 1.6 collective-permute-done.7.refs_1_
  77.5 8.7 %mix.4 = (bf16[512,4096]{1,0:T(8,128)(2,1)}, bf16[16,128,512]{2,1,0:T(8,128)(2,1)S(1)}, f32[8,16,16,256]{3,2,1,0:T(8,128)S(1)}, bf16[8,16,16,256]{3,2,1,0:T(8,12...) custom-call(s32[2]{0:T(128)S(1)} %pad_add_fusion.ids_ref, ...), custom_call_target="tpu_custom_call", output_to_operand_aliasing={{0}: (8, {}), {1}: (9, {}), {2}: (10, {}), {3}: (11, {}), {... | custom-call | flops 1 | bytes 1 | tf_op jit(solution)/shard_map/mix/pallas_call | solution.py:60
  86.2 1.7 collective-permute-done.6.refs_1_
  87.9 6.6 %mix.5 = (bf16[512,4096]{1,0:T(8,128)(2,1)}, bf16[16,128,512]{2,1,0:T(8,128)(2,1)S(1)}, f32[8,16,16,256]{3,2,1,0:T(8,128)S(1)}, bf16[8,16,16,256]{3,2,1,0:T(8,12...) custom-call(s32[2]{0:T(128)S(1)} %pad_add_fusion.ids_ref, ...), custom_call_target="tpu_custom_call", output_to_operand_aliasing={{0}: (8, {}), {1}: (9, {}), {2}: (10, {}), {3}: (11, {}), {... | custom-call | flops 1 | bytes 1 | tf_op jit(solution)/shard_map/mix/pallas_call | solution.py:60
  94.5 1.7 collective-permute-start.11
  96.2 1.0 collective-permute-done.12
  97.3 1.7 collective-permute-start.13
  99.1 1.5 collective-permute-start.10
  100.6 10.8 %collective-permute-done.13 = bf16[4,16,16,256]{3,2,1,0:T(8,128)(2,1)S(1)} collective-permute-done((bf16[4,16,16,256]{3,2,1,0:T(8,128)(2,1)S(1)}, bf16[4,16,16,256]{3,2,1,0:T(8,128)(2,1)S(1)}, u32[]{:S(2)}, u32[]{:S(2)}) %collective-permute-start.13) | collective-permute-done | bytes 524320 | tf_op jit(solution)/shard_map/ppermute | solution.py:124
  111.5 3.3 %collective-permute-done.11.refs_1_ = bf16[16,48,512]{2,1,0:T(8,128)(2,1)S(1)} collective-permute-done((bf16[16,48,512]{2,1,0:T(8,128)(2,1)S(1)}, bf16[16,48,512]{2,1,0:T(8,128)(2,1)S(1)}, u32[]{:S(2)}, u32[]{:S(2)}) %collective-permute-start.11) | collective-permute-done | bytes 786464 | tf_op jit(solution)/shard_map/ppermute | solution.py:431
  114.8 5.1 %fold.3 = (bf16[512,4096]{1,0:T(8,128)(2,1)}, f32[8,6,16,256]{3,2,1,0:T(8,128)S(1)}, bf16[8,6,16,256]{3,2,1,0:T(8,128)(2,1)S(1)}) custom-call(s32[2]{0:T(128)S(1)} %pad_add_fusion.ids_ref, bf16[16,128,512]{2,1,0:T(8,128)(2,1)S(1)} %get-tuple-element.55.refs_0_, bf16[16,48,512]{2,1,0:T(8,128)(2,1)S(1)} %collective-permute-done.11.refs_1_, ...), custom_call_target="tpu_custom_call" | custom-call | flops 1 | bytes 1 | tf_op jit(solution)/shard_map/fold/pallas_call | solution.py:60
  119.9 1.7 collective-permute-start.9
  121.6 1.4 collective-permute-start.17
  123.1 2.9 %collective-permute-start.15 = (bf16[1,16,16,256]{3,2,1,0:T(8,128)(2,1)S(1)}, bf16[1,16,16,256]{3,2,1,0:T(8,128)(2,1)S(1)}, u32[]{:S(2)}, u32[]{:S(2)}) collective-permute-start(bf16[1,16,16,256]{3,2,1,0:T(8,128)(2,1)S(1)} %get-tuple-element.72.refs_11_), channel_id=1, source_target_pairs={{0,8},{2,10},{4,12},{6,14},{8,0},{10,2},{12,4},{14,6},{16,24},{18,... | collective-permute-start | bytes 393224 | tf_op jit(solution)/shard_map/ppermute | solution.py:124
  126.1 5.6 %collective-permute-done.10.refs_1_ = bf16[16,48,512]{2,1,0:T(8,128)(2,1)S(1)} collective-permute-done((bf16[16,48,512]{2,1,0:T(8,128)(2,1)S(1)}, bf16[16,48,512]{2,1,0:T(8,128)(2,1)S(1)}, u32[]{:S(2)}, u32[]{:S(2)}) %collective-permute-start.10) | collective-permute-done | bytes 786464 | tf_op jit(solution)/shard_map/ppermute | solution.py:431
  131.7 1.7 collective-permute-start.18
  133.4 5.1 %fold.4 = (bf16[512,4096]{1,0:T(8,128)(2,1)}, f32[8,6,16,256]{3,2,1,0:T(8,128)S(1)}, bf16[8,6,16,256]{3,2,1,0:T(8,128)(2,1)S(1)}) custom-call(s32[2]{0:T(128)S(1)} %pad_add_fusion.ids_ref, bf16[16,128,512]{2,1,0:T(8,128)(2,1)S(1)} %get-tuple-element.55.refs_0_, ...), custom_call_target="tpu_custom_call", output_to_operand_aliasing={{0}: (12, {})} | custom-call | flops 1 | bytes 1 | tf_op jit(solution)/shard_map/fold/pallas_call | solution.py:60
  138.8 1.4 collective-permute-done.20
  140.3 0.4 collective-permute-start.21
  140.7 3.3 %collective-permute-done.19 = bf16[2,6,16,256]{3,2,1,0:T(8,128)(2,1)S(1)} collective-permute-done((bf16[2,6,16,256]{3,2,1,0:T(8,128)(2,1)S(1)}, bf16[2,6,16,256]{3,2,1,0:T(8,128)(2,1)S(1)}, u32[]{:S(2)}, u32[]{:S(2)}) %collective-permute-start.19) | collective-permute-done | bytes 98336 | tf_op jit(solution)/shard_map/ppermute | solution.py:124
  144.0 3.3 %collective-permute-done.21 = bf16[4,6,16,256]{3,2,1,0:T(8,128)(2,1)S(1)} collective-permute-done((bf16[4,6,16,256]{3,2,1,0:T(8,128)(2,1)S(1)}, bf16[4,6,16,256]{3,2,1,0:T(8,128)(2,1)S(1)}, u32[]{:S(2)}, u32[]{:S(2)}) %collective-permute-start.21) | collective-permute-done | bytes 196640 | tf_op jit(solution)/shard_map/ppermute | solution.py:124
  147.3 3.9 %fold.5 = (bf16[512,4096]{1,0:T(8,128)(2,1)}, f32[8,4,16,256]{3,2,1,0:T(8,128)S(1)}, bf16[8,4,16,256]{3,2,1,0:T(8,128)(2,1)S(1)}) custom-call(s32[2]{0:T(128)S(1)} %pad_add_fusion.ids_ref, bf16[16,128,512]{2,1,0:T(8,128)(2,1)S(1)} %get-tuple-element.55.refs_0_, ...), custom_call_target="tpu_custom_call", output_to_operand_aliasing={{0}: (12, {})} | custom-call | flops 1 | bytes 1 | tf_op jit(solution)/shard_map/fold/pallas_call | solution.py:60
  151.2 0.7 collective-permute-start.22
  151.9 0.8 collective-permute-done.24
  152.8 0.4 collective-permute-start.25
  153.2 3.2 %collective-permute-done.22 = bf16[2,6,16,256]{3,2,1,0:T(8,128)(2,1)S(1)} collective-permute-done((bf16[2,6,16,256]{3,2,1,0:T(8,128)(2,1)S(1)}, bf16[2,6,16,256]{3,2,1,0:T(8,128)(2,1)S(1)}, u32[]{:S(2)}, u32[]{:S(2)}) %collective-permute-start.22) | collective-permute-done | bytes 98336 | tf_op jit(solution)/shard_map/ppermute | solution.py:124
  156.4 1.9 %collective-permute-done.25 = bf16[4,4,16,256]{3,2,1,0:T(8,128)(2,1)S(1)} collective-permute-done((bf16[4,4,16,256]{3,2,1,0:T(8,128)(2,1)S(1)}, bf16[4,4,16,256]{3,2,1,0:T(8,128)(2,1)S(1)}, u32[]{:S(2)}, u32[]{:S(2)}) %collective-permute-start.25) | collective-permute-done | bytes 131104 | tf_op jit(solution)/shard_map/ppermute | solution.py:124
  158.4 0.7 collective-permute-start.26
  159.1 1.4 collective-permute-start.23
  160.6 2.9 %collective-permute-done.26 = bf16[2,4,16,256]{3,2,1,0:T(8,128)(2,1)S(1)} collective-permute-done((bf16[2,4,16,256]{3,2,1,0:T(8,128)(2,1)S(1)}, bf16[2,4,16,256]{3,2,1,0:T(8,128)(2,1)S(1)}, u32[]{:S(2)}, u32[]{:S(2)}) %collective-permute-start.26) | collective-permute-done | bytes 65568 | tf_op jit(solution)/shard_map/ppermute | solution.py:124
  163.8 2.8 %collective-permute-done.23 = bf16[1,12,16,256]{3,2,1,0:T(8,128)(2,1)S(1)} collective-permute-done((bf16[1,12,16,256]{3,2,1,0:T(8,128)(2,1)S(1)}, bf16[1,12,16,256]{3,2,1,0:T(8,128)(2,1)S(1)}, u32[]{:S(2)}, u32[]{:S(2)}) %collective-permute-start.23) | collective-permute-done | bytes 98336 | tf_op jit(solution)/shard_map/ppermute | solution.py:124
  166.8 1.9 %collective-permute-done.27 = bf16[1,4,16,256]{3,2,1,0:T(8,128)(2,1)S(1)} collective-permute-done((bf16[1,4,16,256]{3,2,1,0:T(8,128)(2,1)S(1)}, bf16[1,4,16,256]{3,2,1,0:T(8,128)(2,1)S(1)}, u32[]{:S(2)}, u32[]{:S(2)}) %collective-permute-start.27) | collective-permute-done | bytes 32800 | tf_op jit(solution)/shard_map/ppermute | solution.py:124
  168.7 0.7 pad_maximum_fusion.1
  (41 shorter events, 1.8 us)
Async XLA Ops:
  7.2 52.9 %all-gather.3.cloned.1.call-start = ((), (), s32[]{:S(2)}) async-start(), calls=%async_computation | async-start | bytes 3342336 | tf_op jit(solution)/shard_map/all_gather | solution.py:436
  9.7 7.7 %collective-permute-start.2 = (bf16[1,16,16,128]{3,2,1,0:T(8,128)(2,1)S(1)}, bf16[1,16,16,128]{3,2,1,0:T(8,128)(2,1)S(1)}, u32[]{:S(2)}, u32[]{:S(2)}) collective-permute-start(bf16[1,16,16,128]{3,2,1,0:T(8,128)(2,1)S(1)} %get-tuple-element.73), channel_id=1, source_target_pairs={{0,24},{2,26},{4,28},{6,30},{8,16},{10,18},{12,20},{14,22},{16,8},... | collective-permute-start | bytes 196616 | tf_op jit(solution)/shard_map/ppermute | solution.py:124
  14.9 5.6 %collective-permute-start.1 = (bf16[1,16,16,128]{3,2,1,0:T(8,128)(2,1)S(1)}, bf16[1,16,16,128]{3,2,1,0:T(8,128)(2,1)S(1)}, u32[]{:S(2)}, u32[]{:S(2)}) collective-permute-start(bf16[1,16,16,128]{3,2,1,0:T(8,128)(2,1)S(1)} %get-tuple-element.73), channel_id=1, source_target_pairs={{0,16},{2,18},{4,20},{6,22},{8,24},{10,26},{12,28},{14,30},{16,0},... | collective-permute-start | bytes 196616 | tf_op jit(solution)/shard_map/ppermute | solution.py:124
  14.9 5.6 %collective-permute-start = (bf16[1,16,16,128]{3,2,1,0:T(8,128)(2,1)S(1)}, bf16[1,16,16,128]{3,2,1,0:T(8,128)(2,1)S(1)}, u32[]{:S(2)}, u32[]{:S(2)}) collective-permute-start(bf16[1,16,16,128]{3,2,1,0:T(8,128)(2,1)S(1)} %get-tuple-element.73), channel_id=1, source_target_pairs={{0,8},{2,10},{4,12},{6,14},{8,0},{10,2},{12,4},{14,6},{16,24},{18,... | collective-permute-start | bytes 196616 | tf_op jit(solution)/shard_map/ppermute | solution.py:124
  20.5 10.0 %collective-permute-start.3 = (bf16[4,16,16,128]{3,2,1,0:T(8,128)(2,1)S(1)}, bf16[4,16,16,128]{3,2,1,0:T(8,128)(2,1)S(1)}, u32[]{:S(2)}, u32[]{:S(2)}) collective-permute-start(bf16[4,16,16,128]{3,2,1,0:T(8,128)(2,1)S(1)} %pad_maximum_fusion.refs_2_.refs_7_), channel_id=1, source_target_pairs={{0,4},{2,6},{4,0},{6,2},{8,12},{10,14},{12,8},{14,10},{16,20},{18,... | collective-permute-start | bytes 786440 | tf_op jit(solution)/shard_map/ppermute | solution.py:124
  22.1 8.6 %collective-permute-start.4 = (bf16[4,16,16,128]{3,2,1,0:T(8,128)(2,1)S(1)}, bf16[4,16,16,128]{3,2,1,0:T(8,128)(2,1)S(1)}, u32[]{:S(2)}, u32[]{:S(2)}) collective-permute-start(bf16[4,16,16,128]{3,2,1,0:T(8,128)(2,1)S(1)} %pad_maximum_fusion.refs_2_.refs_7_), channel_id=1, source_target_pairs={{0,2},{2,0},{4,6},{6,4},{8,10},{10,8},{12,14},{14,12},{16,18},{18,... | collective-permute-start | bytes 786440 | tf_op jit(solution)/shard_map/ppermute | solution.py:124
  30.6 1.5 collective-permute-start.5
  40.0 27.1 %collective-permute-start.8 = (bf16[6,128,512]{2,1,0:T(8,128)(2,1)}, bf16[6,128,512]{2,1,0:T(8,128)(2,1)S(1)}, u32[]{:S(2)}, u32[]{:S(2)}) collective-permute-start(bf16[6,128,512]{2,1,0:T(8,128)(2,1)} %get-tuple-element.39), channel_id=1, source_target_pairs={{0,1},{1,0},{2,3},{3,2},{4,5},{5,4},{6,7},{7,6},{8,9},{9,8},{10,11... | collective-permute-start | bytes 2359304 | tf_op jit(solution)/shard_map/ppermute | solution.py:431
  41.7 35.8 %collective-permute-start.7 = (bf16[6,128,512]{2,1,0:T(8,128)(2,1)}, bf16[6,128,512]{2,1,0:T(8,128)(2,1)S(1)}, u32[]{:S(2)}, u32[]{:S(2)}) collective-permute-start(bf16[6,128,512]{2,1,0:T(8,128)(2,1)} %get-tuple-element.38), channel_id=1, source_target_pairs={{0,1},{1,0},{2,3},{3,2},{4,5},{5,4},{6,7},{7,6},{8,9},{9,8},{10,11... | collective-permute-start | bytes 2359304 | tf_op jit(solution)/shard_map/ppermute | solution.py:431
  42.0 45.9 %collective-permute-start.6 = (bf16[4,128,512]{2,1,0:T(8,128)(2,1)}, bf16[4,128,512]{2,1,0:T(8,128)(2,1)S(1)}, u32[]{:S(2)}, u32[]{:S(2)}) collective-permute-start(bf16[4,128,512]{2,1,0:T(8,128)(2,1)} %get-tuple-element.37), channel_id=1, source_target_pairs={{0,1},{1,0},{2,3},{3,2},{4,5},{5,4},{6,7},{7,6},{8,9},{9,8},{10,11... | collective-permute-start | bytes 1572872 | tf_op jit(solution)/shard_map/ppermute | solution.py:431
  94.5 2.7 %collective-permute-start.12 = (bf16[8,16,16,256]{3,2,1,0:T(8,128)(2,1)S(1)}, bf16[8,16,16,256]{3,2,1,0:T(8,128)(2,1)S(1)}, u32[]{:S(2)}, u32[]{:S(2)}) collective-permute-start(bf16[8,16,16,256]{3,2,1,0:T(8,128)(2,1)S(1)} %get-tuple-element.60), channel_id=1, source_target_pairs={{0,2},{2,0},{4,6},{6,4},{8,10},{10,8},{12,14},{14,12},{16,18},{18,... | collective-permute-start | bytes 3145736 | tf_op jit(solution)/shard_map/ppermute | solution.py:124
  94.5 20.3 %collective-permute-start.11 = (bf16[16,48,512]{2,1,0:T(8,128)(2,1)S(1)}, bf16[16,48,512]{2,1,0:T(8,128)(2,1)S(1)}, u32[]{:S(2)}, u32[]{:S(2)}) collective-permute-start(bf16[16,48,512]{2,1,0:T(8,128)(2,1)S(1)} %get-tuple-element.58), channel_id=1, source_target_pairs={{0,1},{1,0},{2,3},{3,2},{4,5},{5,4},{6,7},{7,6},{8,9},{9,8},{10,11... | collective-permute-start | bytes 2359304 | tf_op jit(solution)/shard_map/ppermute | solution.py:431
  97.3 14.0 %collective-permute-start.13 = (bf16[4,16,16,256]{3,2,1,0:T(8,128)(2,1)S(1)}, bf16[4,16,16,256]{3,2,1,0:T(8,128)(2,1)S(1)}, u32[]{:S(2)}, u32[]{:S(2)}) collective-permute-start(bf16[4,16,16,256]{3,2,1,0:T(8,128)(2,1)S(1)} %add_convert_fusion), channel_id=1, source_target_pairs={{0,4},{2,6},{4,0},{6,2},{8,12},{10,14},{12,8},{14,10},{16,20},{18,... | collective-permute-start | bytes 1572872 | tf_op jit(solution)/shard_map/ppermute | solution.py:124
  99.1 32.6 %collective-permute-start.10 = (bf16[16,48,512]{2,1,0:T(8,128)(2,1)S(1)}, bf16[16,48,512]{2,1,0:T(8,128)(2,1)S(1)}, u32[]{:S(2)}, u32[]{:S(2)}) collective-permute-start(bf16[16,48,512]{2,1,0:T(8,128)(2,1)S(1)} %get-tuple-element.57), channel_id=1, source_target_pairs={{0,1},{1,0},{2,3},{3,2},{4,5},{5,4},{6,7},{7,6},{8,9},{9,8},{10,11... | collective-permute-start | bytes 2359304 | tf_op jit(solution)/shard_map/ppermute | solution.py:431
  119.9 3.1 %collective-permute-start.14 = (bf16[8,6,16,256]{3,2,1,0:T(8,128)(2,1)S(1)}, bf16[8,6,16,256]{3,2,1,0:T(8,128)(2,1)S(1)}, u32[]{:S(2)}, u32[]{:S(2)}) collective-permute-start(bf16[8,6,16,256]{3,2,1,0:T(8,128)(2,1)S(1)} %get-tuple-element.63), channel_id=1, source_target_pairs={{0,2},{2,0},{4,6},{6,4},{8,10},{10,8},{12,14},{14,12},{16,18},{18,... | collective-permute-start | bytes 1179656 | tf_op jit(solution)/shard_map/ppermute | solution.py:124
  119.9 27.4 %collective-permute-start.9 = (bf16[16,32,512]{2,1,0:T(8,128)(2,1)S(1)}, bf16[16,32,512]{2,1,0:T(8,128)(2,1)S(1)}, u32[]{:S(2)}, u32[]{:S(2)}) collective-permute-start(bf16[16,32,512]{2,1,0:T(8,128)(2,1)S(1)} %get-tuple-element.56), channel_id=1, source_target_pairs={{0,1},{1,0},{2,3},{3,2},{4,5},{5,4},{6,7},{7,6},{8,9},{9,8},{10,11... | collective-permute-start | bytes 1572872 | tf_op jit(solution)/shard_map/ppermute | solution.py:431
  121.6 16.9 %collective-permute-start.17 = (bf16[1,16,16,256]{3,2,1,0:T(8,128)(2,1)S(1)}, bf16[1,16,16,256]{3,2,1,0:T(8,128)(2,1)S(1)}, u32[]{:S(2)}, u32[]{:S(2)}) collective-permute-start(bf16[1,16,16,256]{3,2,1,0:T(8,128)(2,1)S(1)} %get-tuple-element.70.refs_13_), channel_id=1, source_target_pairs={{0,24},{2,26},{4,28},{6,30},{8,16},{10,18},{12,20},{14,22},{16,8},... | collective-permute-start | bytes 393224 | tf_op jit(solution)/shard_map/ppermute | solution.py:124
  123.1 15.4 %collective-permute-start.16 = (bf16[1,16,16,256]{3,2,1,0:T(8,128)(2,1)S(1)}, bf16[1,16,16,256]{3,2,1,0:T(8,128)(2,1)S(1)}, u32[]{:S(2)}, u32[]{:S(2)}) collective-permute-start(bf16[1,16,16,256]{3,2,1,0:T(8,128)(2,1)S(1)} %get-tuple-element.71.refs_12_), channel_id=1, source_target_pairs={{0,16},{2,18},{4,20},{6,22},{8,24},{10,26},{12,28},{14,30},{16,0},... | collective-permute-start | bytes 393224 | tf_op jit(solution)/shard_map/ppermute | solution.py:124
  123.1 15.4 %collective-permute-start.15 = (bf16[1,16,16,256]{3,2,1,0:T(8,128)(2,1)S(1)}, bf16[1,16,16,256]{3,2,1,0:T(8,128)(2,1)S(1)}, u32[]{:S(2)}, u32[]{:S(2)}) collective-permute-start(bf16[1,16,16,256]{3,2,1,0:T(8,128)(2,1)S(1)} %get-tuple-element.72.refs_11_), channel_id=1, source_target_pairs={{0,8},{2,10},{4,12},{6,14},{8,0},{10,2},{12,4},{14,6},{16,24},{18,... | collective-permute-start | bytes 393224 | tf_op jit(solution)/shard_map/ppermute | solution.py:124
  131.7 7.0 %collective-permute-start.18 = (bf16[4,6,16,256]{3,2,1,0:T(8,128)(2,1)S(1)}, bf16[4,6,16,256]{3,2,1,0:T(8,128)(2,1)S(1)}, u32[]{:S(2)}, u32[]{:S(2)}) collective-permute-start(bf16[4,6,16,256]{3,2,1,0:T(8,128)(2,1)S(1)} %add_convert_fusion.2.refs_12_), channel_id=1, source_target_pairs={{0,4},{2,6},{4,0},{6,2},{8,12},{10,14},{12,8},{14,10},{16,20},{18,... | collective-permute-start | bytes 589832 | tf_op jit(solution)/shard_map/ppermute | solution.py:124
  138.5 1.7 collective-permute-start.20
  138.6 12.6 %copy-start = (f32[16,16,256]{2,1,0:T(8,128)}, f32[16,16,256]{2,1,0:T(8,128)S(1)}, u32[]{:S(2)}) copy-start(f32[16,16,256]{2,1,0:T(8,128)S(1)} %multiply_bitcast_fusion.refs_12_) | copy-start | bytes 786436
  138.7 5.2 %collective-permute-start.19 = (bf16[2,6,16,256]{3,2,1,0:T(8,128)(2,1)S(1)}, bf16[2,6,16,256]{3,2,1,0:T(8,128)(2,1)S(1)}, u32[]{:S(2)}, u32[]{:S(2)}) collective-permute-start(bf16[2,6,16,256]{3,2,1,0:T(8,128)(2,1)S(1)} %add_convert_fusion.8), channel_id=1, source_target_pairs={{0,8},{2,10},{4,12},{6,14},{8,0},{10,2},{12,4},{14,6},{16,24},{18,... | collective-permute-start | bytes 294920 | tf_op jit(solution)/shard_map/ppermute | solution.py:124
  140.3 7.0 %collective-permute-start.21 = (bf16[4,6,16,256]{3,2,1,0:T(8,128)(2,1)S(1)}, bf16[4,6,16,256]{3,2,1,0:T(8,128)(2,1)S(1)}, u32[]{:S(2)}, u32[]{:S(2)}) collective-permute-start(bf16[4,6,16,256]{3,2,1,0:T(8,128)(2,1)S(1)} %add_convert_fusion.1), channel_id=1, source_target_pairs={{0,4},{2,6},{4,0},{6,2},{8,12},{10,14},{12,8},{14,10},{16,20},{18,... | collective-permute-start | bytes 589832 | tf_op jit(solution)/shard_map/ppermute | solution.py:124
  151.2 1.5 collective-permute-start.24
  151.2 5.2 %collective-permute-start.22 = (bf16[2,6,16,256]{3,2,1,0:T(8,128)(2,1)S(1)}, bf16[2,6,16,256]{3,2,1,0:T(8,128)(2,1)S(1)}, u32[]{:S(2)}, u32[]{:S(2)}) collective-permute-start(bf16[2,6,16,256]{3,2,1,0:T(8,128)(2,1)S(1)} %add_convert_fusion.7.refs_14_), channel_id=1, source_target_pairs={{0,8},{2,10},{4,12},{6,14},{8,0},{10,2},{12,4},{14,6},{16,24},{18,... | collective-permute-start | bytes 294920 | tf_op jit(solution)/shard_map/ppermute | solution.py:124
  152.8 5.6 %collective-permute-start.25 = (bf16[4,4,16,256]{3,2,1,0:T(8,128)(2,1)S(1)}, bf16[4,4,16,256]{3,2,1,0:T(8,128)(2,1)S(1)}, u32[]{:S(2)}, u32[]{:S(2)}) collective-permute-start(bf16[4,4,16,256]{3,2,1,0:T(8,128)(2,1)S(1)} %add_convert_fusion.3), channel_id=1, source_target_pairs={{0,4},{2,6},{4,0},{6,2},{8,12},{10,14},{12,8},{14,10},{16,20},{18,... | collective-permute-start | bytes 393224 | tf_op jit(solution)/shard_map/ppermute | solution.py:124
  158.4 5.1 %collective-permute-start.26 = (bf16[2,4,16,256]{3,2,1,0:T(8,128)(2,1)S(1)}, bf16[2,4,16,256]{3,2,1,0:T(8,128)(2,1)S(1)}, u32[]{:S(2)}, u32[]{:S(2)}) collective-permute-start(bf16[2,4,16,256]{3,2,1,0:T(8,128)(2,1)S(1)} %add_convert_fusion.9), channel_id=1, source_target_pairs={{0,8},{2,10},{4,12},{6,14},{8,0},{10,2},{12,4},{14,6},{16,24},{18,... | collective-permute-start | bytes 196616 | tf_op jit(solution)/shard_map/ppermute | solution.py:124
  159.1 7.5 %collective-permute-start.23 = (bf16[1,12,16,256]{3,2,1,0:T(8,128)(2,1)S(1)}, bf16[1,12,16,256]{3,2,1,0:T(8,128)(2,1)S(1)}, u32[]{:S(2)}, u32[]{:S(2)}) collective-permute-start(bf16[1,12,16,256]{3,2,1,0:T(8,128)(2,1)S(1)} %pad_maximum_fusion.3), channel_id=1, source_target_pairs={{0,16},{2,18},{4,20},{6,22},{8,24},{10,26},{12,28},{14,30},{16,0},... | collective-permute-start | bytes 294920 | tf_op jit(solution)/shard_map/ppermute | solution.py:124
  163.5 5.1 %collective-permute-start.27 = (bf16[1,4,16,256]{3,2,1,0:T(8,128)(2,1)S(1)}, bf16[1,4,16,256]{3,2,1,0:T(8,128)(2,1)S(1)}, u32[]{:S(2)}, u32[]{:S(2)}) collective-permute-start(bf16[1,4,16,256]{3,2,1,0:T(8,128)(2,1)S(1)} %add_convert_fusion.12), channel_id=1, source_target_pairs={{0,16},{2,18},{4,20},{6,22},{8,24},{10,26},{12,28},{14,30},{16,0},... | collective-permute-start | bytes 98312 | tf_op jit(solution)/shard_map/ppermute | solution.py:124
Sparse Core Ops, SparseCore 0:
  10.9 49.2 all-gather.2

commit v2 on v0

--- a/solution.py
+++ b/solution.py
@@ -12,7 +12,7 @@
 F32 = jnp.float32
 ROOT_HALF = math.sqrt(0.5)
 DENSITY = 1.0 / math.sqrt(2.0 * math.pi)
-JOINED = (True, False, False, False)
+JOINED = (True, False, False, True)
 TIES = {0: ((0, 2),), 1: ((1, 1),), 2: ((0, 3), (1, 3), (2, 2))}
 VMEM = 20 * 1024 * 1024
 LARGE = 1 << 20

time: 177 us -> 174 us (0.983)
  waiting for transfers between devices: 75.4 us -> 72.1 us
    ppermute x23 -> x24, waiting for transfers between devices: 46.8 us -> 43.5 us  [swap(): lax.ppermute(array, 'dp', [(at, at ^ mask) for at in range(self.size)])]
    ppermute x23 -> x24, starting transfers between devices: 20.5 us -> 21.3 us  [swap(): lax.ppermute(array, 'dp', [(at, at ^ mask) for at in range(self.size)])]
  transfers between devices with their start and end apart: 30 -> 31, of which waited for: 21 -> 21; matrix products, arithmetic and copies ran while one was open for 1% -> 1% of each run, Pallas kernels for 24% -> 27%
where the time goes in v2:
time: 174 us
  waiting for transfers between devices  72.1 us (41%)
  Pallas kernels  53.1 us (31%)
  starting transfers between devices  29.9 us (17%)
  between operations  14.2 us (8%)
  other arithmetic  3.33 us (2%)
    pallas_call x8, Pallas kernels, call(): pl.pallas_call(body, grid_spec=pltpu.PrefetchScalarGridSpec(num_scalar_pr...  53.1 us
    ppermute x24, waiting for transfers between devices, swap(): lax.ppermute(array, 'dp', [(at, at ^ mask) for at in range(self.size)])  43.5 us
    ppermute x24, starting transfers between devices, swap(): lax.ppermute(array, 'dp', [(at, at ^ mask) for at in range(self.size)])  21.3 us
    all_gather x1, waiting for transfers between devices, gather_plain(): whole = lax.all_gather(shard, 'dp', axis=0, tiled=False)  16.3 us
    ppermute x6, waiting for transfers between devices, send(): lax.ppermute(array, 'mp', [(at, (at + shift) % group) for at in range(gro...  12.2 us
    ppermute x6, starting transfers between devices, send(): lax.ppermute(array, 'mp', [(at, (at + shift) % group) for at in range(gro...  8.55 us
  transfers between devices with their start and end apart: 31, of which 21 were waited for; matrix products, arithmetic and copies ran while one was open for 1% of the time, Pallas kernels for 27%

profile of v2, /device:TPU:0, one launch (start us, length us, event | category | flops | bytes accessed | tf_op | source)
XLA Modules:
  0.0 173.5 jit_solution(17259200874744453592)
XLA Ops:
  7.2 0.9 dynamic-slice_bitcast_fusion
  8.1 1.6 pad_maximum_fusion.2
  9.7 5.1 %collective-permute-start.2 = (bf16[1,16,16,128]{3,2,1,0:T(8,128)(2,1)S(1)}, bf16[1,16,16,128]{3,2,1,0:T(8,128)(2,1)S(1)}, u32[]{:S(2)}, u32[]{:S(2)}) collective-permute-start(bf16[1,16,16,128]{3,2,1,0:T(8,128)(2,1)S(1)} %get-tuple-element.76), channel_id=1, source_target_pairs={{0,24},{2,26},{4,28},{6,30},{8,16},{10,18},{12,20},{14,22},{16,8},... | collective-permute-start | bytes 196616 | tf_op jit(solution)/shard_map/ppermute | solution.py:123
  14.9 0.6 collective-permute-start
  15.5 1.9 %collective-permute-done.2 = bf16[1,16,16,128]{3,2,1,0:T(8,128)(2,1)S(1)} collective-permute-done((bf16[1,16,16,128]{3,2,1,0:T(8,128)(2,1)S(1)}, bf16[1,16,16,128]{3,2,1,0:T(8,128)(2,1)S(1)}, u32[]{:S(2)}, u32[]{:S(2)}) %collective-permute-start.2) | collective-permute-done | bytes 65568 | tf_op jit(solution)/shard_map/ppermute | solution.py:123
  17.4 3.0 %collective-permute-done.1 = bf16[1,16,16,128]{3,2,1,0:T(8,128)(2,1)S(1)} collective-permute-done((bf16[1,16,16,128]{3,2,1,0:T(8,128)(2,1)S(1)}, bf16[1,16,16,128]{3,2,1,0:T(8,128)(2,1)S(1)}, u32[]{:S(2)}, u32[]{:S(2)}) %collective-permute-start.1) | collective-permute-done | bytes 65568 | tf_op jit(solution)/shard_map/ppermute | solution.py:123
  20.5 1.6 collective-permute-start.3
  22.1 8.5 %collective-permute-done.3.refs_3_.refs_8_ = bf16[4,16,16,128]{3,2,1,0:T(8,128)(2,1)S(1)} collective-permute-done((bf16[4,16,16,128]{3,2,1,0:T(8,128)(2,1)S(1)}, bf16[4,16,16,128]{3,2,1,0:T(8,128)(2,1)S(1)}, u32[]{:S(2)}, u32[]{:S(2)}) %collective-permute-start.3) | collective-permute-done | bytes 262176 | tf_op jit(solution)/shard_map/ppermute | solution.py:123
  30.6 1.5 collective-permute-done.5.refs_5_.refs_10_
  32.1 7.9 %expand.3 = (bf16[6,128,512]{2,1,0:T(8,128)(2,1)}, bf16[6,128,512]{2,1,0:T(8,128)(2,1)}, bf16[4,128,512]{2,1,0:T(8,128)(2,1)}) custom-call(s32[2]{0:T(128)S(1)} %pad_add_fusion.ids_ref, bf16[512,4096]{1,0:T(8,128)(2,1)} %refs_3_.11, bf16[512,4096]{1,0:T(8,128)(2,1)} %refs_3_.11, bf16[4,16,16,128]{3,2,1,0:T(8,128)(2,1)S(1)} %pad_maximum_fusion.refs_2_.refs_7_, ...), custom_call_target="tpu_custom_call" | custom-call | flops 1 | bytes 1 | tf_op jit(solution)/shard_map/expand/pallas_call | solution.py:59
  40.0 1.7 collective-permute-start.8
  42.1 1.7 collective-permute-start.6
  43.8 16.3 %all-gather.3.cloned.1.call-done = bf16[256,16,384]{2,1,0:T(8,128)(2,1)} async-done(((bf16[16,16,384]{2,1,0:T(8,128)(2,1)}), bf16[256,16,384]{2,1,0:T(8,128)(2,1)}) %all-gather.3.cloned.1.call-update) | async-done | bytes 3145744 | tf_op jit(solution)/shard_map/all_gather | solution.py:424
  60.1 7.0 %expand.2.refs_0_ = bf16[16,128,512]{2,1,0:T(8,128)(2,1)S(1)} custom-call(s32[2]{0:T(128)S(1)} %pad_add_fusion.ids_ref, bf16[512,4096]{1,0:T(8,128)(2,1)} %refs_3_.11, bf16[512,4096]{1,0:T(8,128)(2,1)} %refs_3_.11, bf16[16,16,16,384]{3,2,1,0:T(8,128)(2,1)} %bitcast.13), custom_call_target="tpu_custom_call" | custom-call | flops 1 | bytes 1 | tf_op jit(solution)/shard_map/expand/pallas_call | solution.py:59
  67.1 8.7 %mix.3 = (bf16[512,4096]{1,0:T(8,128)(2,1)}, bf16[16,128,512]{2,1,0:T(8,128)(2,1)S(1)}, f32[8,16,16,256]{3,2,1,0:T(8,128)S(1)}, bf16[8,16,16,256]{3,2,1,0:T(8,12...) custom-call(s32[2]{0:T(128)S(1)} %pad_add_fusion.ids_ref, ...), custom_call_target="tpu_custom_call" | custom-call | flops 1 | bytes 1 | tf_op jit(solution)/shard_map/mix/pallas_call | solution.py:59
  75.9 1.6 collective-permute-done.7.refs_1_
  77.5 8.7 %mix.4 = (bf16[512,4096]{1,0:T(8,128)(2,1)}, bf16[16,128,512]{2,1,0:T(8,128)(2,1)S(1)}, f32[8,16,16,256]{3,2,1,0:T(8,128)S(1)}, bf16[8,16,16,256]{3,2,1,0:T(8,12...) custom-call(s32[2]{0:T(128)S(1)} %pad_add_fusion.ids_ref, ...), custom_call_target="tpu_custom_call", output_to_operand_aliasing={{0}: (8, {}), {1}: (9, {}), {2}: (10, {}), {3}: (11, {}), {... | custom-call | flops 1 | bytes 1 | tf_op jit(solution)/shard_map/mix/pallas_call | solution.py:59
  86.2 1.7 collective-permute-done.6.refs_1_
  87.9 6.6 %mix.5 = (bf16[512,4096]{1,0:T(8,128)(2,1)}, bf16[16,128,512]{2,1,0:T(8,128)(2,1)S(1)}, f32[8,16,16,256]{3,2,1,0:T(8,128)S(1)}, bf16[8,16,16,256]{3,2,1,0:T(8,12...) custom-call(s32[2]{0:T(128)S(1)} %pad_add_fusion.ids_ref, ...), custom_call_target="tpu_custom_call", output_to_operand_aliasing={{0}: (8, {}), {1}: (9, {}), {2}: (10, {}), {3}: (11, {}), {... | custom-call | flops 1 | bytes 1 | tf_op jit(solution)/shard_map/mix/pallas_call | solution.py:59
  94.5 1.7 collective-permute-start.11
  96.2 1.0 collective-permute-done.12
  97.3 1.7 collective-permute-start.13
  99.1 1.5 collective-permute-start.10
  100.6 10.8 %collective-permute-done.13 = bf16[4,16,16,256]{3,2,1,0:T(8,128)(2,1)S(1)} collective-permute-done((bf16[4,16,16,256]{3,2,1,0:T(8,128)(2,1)S(1)}, bf16[4,16,16,256]{3,2,1,0:T(8,128)(2,1)S(1)}, u32[]{:S(2)}, u32[]{:S(2)}) %collective-permute-start.13) | collective-permute-done | bytes 524320 | tf_op jit(solution)/shard_map/ppermute | solution.py:123
  111.5 3.3 %collective-permute-done.11.refs_1_ = bf16[16,48,512]{2,1,0:T(8,128)(2,1)S(1)} collective-permute-done((bf16[16,48,512]{2,1,0:T(8,128)(2,1)S(1)}, bf16[16,48,512]{2,1,0:T(8,128)(2,1)S(1)}, u32[]{:S(2)}, u32[]{:S(2)}) %collective-permute-start.11) | collective-permute-done | bytes 786464 | tf_op jit(solution)/shard_map/ppermute | solution.py:419
  114.8 5.1 %fold.3 = (bf16[512,4096]{1,0:T(8,128)(2,1)}, f32[8,6,16,256]{3,2,1,0:T(8,128)S(1)}, bf16[8,6,16,256]{3,2,1,0:T(8,128)(2,1)S(1)}) custom-call(s32[2]{0:T(128)S(1)} %pad_add_fusion.ids_ref, bf16[16,128,512]{2,1,0:T(8,128)(2,1)S(1)} %get-tuple-element.55.refs_0_, bf16[16,48,512]{2,1,0:T(8,128)(2,1)S(1)} %collective-permute-done.11.refs_1_, ...), custom_call_target="tpu_custom_call" | custom-call | flops 1 | bytes 1 | tf_op jit(solution)/shard_map/fold/pallas_call | solution.py:59
  120.0 1.7 collective-permute-start.9
  121.6 1.4 collective-permute-start.17
  123.1 2.9 %collective-permute-start.15 = (bf16[1,16,16,256]{3,2,1,0:T(8,128)(2,1)S(1)}, bf16[1,16,16,256]{3,2,1,0:T(8,128)(2,1)S(1)}, u32[]{:S(2)}, u32[]{:S(2)}) collective-permute-start(bf16[1,16,16,256]{3,2,1,0:T(8,128)(2,1)S(1)} %get-tuple-element.72.refs_11_), channel_id=1, source_target_pairs={{0,8},{2,10},{4,12},{6,14},{8,0},{10,2},{12,4},{14,6},{16,24},{18,... | collective-permute-start | bytes 393224 | tf_op jit(solution)/shard_map/ppermute | solution.py:123
  126.1 5.6 %collective-permute-done.10.refs_1_ = bf16[16,48,512]{2,1,0:T(8,128)(2,1)S(1)} collective-permute-done((bf16[16,48,512]{2,1,0:T(8,128)(2,1)S(1)}, bf16[16,48,512]{2,1,0:T(8,128)(2,1)S(1)}, u32[]{:S(2)}, u32[]{:S(2)}) %collective-permute-start.10) | collective-permute-done | bytes 786464 | tf_op jit(solution)/shard_map/ppermute | solution.py:419
  131.7 1.7 collective-permute-start.18
  133.4 5.1 %fold.4 = (bf16[512,4096]{1,0:T(8,128)(2,1)}, f32[8,6,16,256]{3,2,1,0:T(8,128)S(1)}, bf16[8,6,16,256]{3,2,1,0:T(8,128)(2,1)S(1)}) custom-call(s32[2]{0:T(128)S(1)} %pad_add_fusion.ids_ref, bf16[16,128,512]{2,1,0:T(8,128)(2,1)S(1)} %get-tuple-element.55.refs_0_, ...), custom_call_target="tpu_custom_call", output_to_operand_aliasing={{0}: (12, {})} | custom-call | flops 1 | bytes 1 | tf_op jit(solution)/shard_map/fold/pallas_call | solution.py:59
  138.8 1.4 collective-permute-done.20
  140.7 3.2 %collective-permute-done.19 = bf16[2,6,16,256]{3,2,1,0:T(8,128)(2,1)S(1)} collective-permute-done((bf16[2,6,16,256]{3,2,1,0:T(8,128)(2,1)S(1)}, bf16[2,6,16,256]{3,2,1,0:T(8,128)(2,1)S(1)}, u32[]{:S(2)}, u32[]{:S(2)}) %collective-permute-start.19) | collective-permute-done | bytes 98336 | tf_op jit(solution)/shard_map/ppermute | solution.py:123
  144.3 3.0 %collective-permute-done.21 = bf16[4,6,16,256]{3,2,1,0:T(8,128)(2,1)S(1)} collective-permute-done((bf16[4,6,16,256]{3,2,1,0:T(8,128)(2,1)S(1)}, bf16[4,6,16,256]{3,2,1,0:T(8,128)(2,1)S(1)}, u32[]{:S(2)}, u32[]{:S(2)}) %collective-permute-start.21) | collective-permute-done | bytes 196640 | tf_op jit(solution)/shard_map/ppermute | solution.py:123
  147.3 3.9 %fold.5 = (bf16[512,4096]{1,0:T(8,128)(2,1)}, f32[8,4,16,256]{3,2,1,0:T(8,128)S(1)}, bf16[8,4,16,256]{3,2,1,0:T(8,128)(2,1)S(1)}) custom-call(s32[2]{0:T(128)S(1)} %pad_add_fusion.ids_ref, bf16[16,128,512]{2,1,0:T(8,128)(2,1)S(1)} %get-tuple-element.55.refs_0_, ...), custom_call_target="tpu_custom_call", output_to_operand_aliasing={{0}: (12, {})} | custom-call | flops 1 | bytes 1 | tf_op jit(solution)/shard_map/fold/pallas_call | solution.py:59
  151.3 0.7 collective-permute-start.23
  152.0 0.8 collective-permute-done.25
  152.8 0.4 collective-permute-start.26
  153.2 3.3 %collective-permute-done.23 = bf16[2,6,16,256]{3,2,1,0:T(8,128)(2,1)S(1)} collective-permute-done((bf16[2,6,16,256]{3,2,1,0:T(8,128)(2,1)S(1)}, bf16[2,6,16,256]{3,2,1,0:T(8,128)(2,1)S(1)}, u32[]{:S(2)}, u32[]{:S(2)}) %collective-permute-start.23) | collective-permute-done | bytes 98336 | tf_op jit(solution)/shard_map/ppermute | solution.py:123
  156.6 0.7 collective-permute-start.24
  157.3 1.1 collective-permute-done.26
  158.4 0.8 collective-permute-start.27
  159.2 1.9 %collective-permute-start.29 = (bf16[1,4,16,256]{3,2,1,0:T(8,128)(2,1)S(1)}, bf16[1,4,16,256]{3,2,1,0:T(8,128)(2,1)S(1)}, u32[]{:S(2)}, u32[]{:S(2)}) collective-permute-start(bf16[1,4,16,256]{3,2,1,0:T(8,128)(2,1)S(1)} %get-tuple-element.74), channel_id=1, source_target_pairs={{0,24},{2,26},{4,28},{6,30},{8,16},{10,18},{12,20},{14,22},{16,8},... | collective-permute-start | bytes 98312 | tf_op jit(solution)/shard_map/ppermute | solution.py:123
  161.1 0.9 collective-permute-start.28
  162.5 2.4 %collective-permute-done.29 = bf16[1,4,16,256]{3,2,1,0:T(8,128)(2,1)S(1)} collective-permute-done((bf16[1,4,16,256]{3,2,1,0:T(8,128)(2,1)S(1)}, bf16[1,4,16,256]{3,2,1,0:T(8,128)(2,1)S(1)}, u32[]{:S(2)}, u32[]{:S(2)}) %collective-permute-start.29) | collective-permute-done | bytes 32800 | tf_op jit(solution)/shard_map/ppermute | solution.py:123
  164.9 1.0 collective-permute-done.28
  166.0 0.7 pad_maximum_fusion.1
  (44 shorter events, 2.8 us)
Async XLA Ops:
  7.2 52.9 %all-gather.3.cloned.1.call-start = ((), (), s32[]{:S(2)}) async-start(), calls=%async_computation | async-start | bytes 3342336 | tf_op jit(solution)/shard_map/all_gather | solution.py:424
  9.7 7.7 %collective-permute-start.2 = (bf16[1,16,16,128]{3,2,1,0:T(8,128)(2,1)S(1)}, bf16[1,16,16,128]{3,2,1,0:T(8,128)(2,1)S(1)}, u32[]{:S(2)}, u32[]{:S(2)}) collective-permute-start(bf16[1,16,16,128]{3,2,1,0:T(8,128)(2,1)S(1)} %get-tuple-element.76), channel_id=1, source_target_pairs={{0,24},{2,26},{4,28},{6,30},{8,16},{10,18},{12,20},{14,22},{16,8},... | collective-permute-start | bytes 196616 | tf_op jit(solution)/shard_map/ppermute | solution.py:123
  14.9 5.6 %collective-permute-start.1 = (bf16[1,16,16,128]{3,2,1,0:T(8,128)(2,1)S(1)}, bf16[1,16,16,128]{3,2,1,0:T(8,128)(2,1)S(1)}, u32[]{:S(2)}, u32[]{:S(2)}) collective-permute-start(bf16[1,16,16,128]{3,2,1,0:T(8,128)(2,1)S(1)} %get-tuple-element.76), channel_id=1, source_target_pairs={{0,16},{2,18},{4,20},{6,22},{8,24},{10,26},{12,28},{14,30},{16,0},... | collective-permute-start | bytes 196616 | tf_op jit(solution)/shard_map/ppermute | solution.py:123
  14.9 5.6 %collective-permute-start = (bf16[1,16,16,128]{3,2,1,0:T(8,128)(2,1)S(1)}, bf16[1,16,16,128]{3,2,1,0:T(8,128)(2,1)S(1)}, u32[]{:S(2)}, u32[]{:S(2)}) collective-permute-start(bf16[1,16,16,128]{3,2,1,0:T(8,128)(2,1)S(1)} %get-tuple-element.76), channel_id=1, source_target_pairs={{0,8},{2,10},{4,12},{6,14},{8,0},{10,2},{12,4},{14,6},{16,24},{18,... | collective-permute-start | bytes 196616 | tf_op jit(solution)/shard_map/ppermute | solution.py:123
  20.5 10.0 %collective-permute-start.3 = (bf16[4,16,16,128]{3,2,1,0:T(8,128)(2,1)S(1)}, bf16[4,16,16,128]{3,2,1,0:T(8,128)(2,1)S(1)}, u32[]{:S(2)}, u32[]{:S(2)}) collective-permute-start(bf16[4,16,16,128]{3,2,1,0:T(8,128)(2,1)S(1)} %pad_maximum_fusion.refs_2_.refs_7_), channel_id=1, source_target_pairs={{0,4},{2,6},{4,0},{6,2},{8,12},{10,14},{12,8},{14,10},{16,20},{18,... | collective-permute-start | bytes 786440 | tf_op jit(solution)/shard_map/ppermute | solution.py:123
  22.1 8.6 %collective-permute-start.4 = (bf16[4,16,16,128]{3,2,1,0:T(8,128)(2,1)S(1)}, bf16[4,16,16,128]{3,2,1,0:T(8,128)(2,1)S(1)}, u32[]{:S(2)}, u32[]{:S(2)}) collective-permute-start(bf16[4,16,16,128]{3,2,1,0:T(8,128)(2,1)S(1)} %pad_maximum_fusion.refs_2_.refs_7_), channel_id=1, source_target_pairs={{0,2},{2,0},{4,6},{6,4},{8,10},{10,8},{12,14},{14,12},{16,18},{18,... | collective-permute-start | bytes 786440 | tf_op jit(solution)/shard_map/ppermute | solution.py:123
  30.6 1.5 collective-permute-start.5
  40.0 27.1 %collective-permute-start.8 = (bf16[6,128,512]{2,1,0:T(8,128)(2,1)}, bf16[6,128,512]{2,1,0:T(8,128)(2,1)S(1)}, u32[]{:S(2)}, u32[]{:S(2)}) collective-permute-start(bf16[6,128,512]{2,1,0:T(8,128)(2,1)} %get-tuple-element.39), channel_id=1, source_target_pairs={{0,1},{1,0},{2,3},{3,2},{4,5},{5,4},{6,7},{7,6},{8,9},{9,8},{10,11... | collective-permute-start | bytes 2359304 | tf_op jit(solution)/shard_map/ppermute | solution.py:419
  41.7 35.7 %collective-permute-start.7 = (bf16[6,128,512]{2,1,0:T(8,128)(2,1)}, bf16[6,128,512]{2,1,0:T(8,128)(2,1)S(1)}, u32[]{:S(2)}, u32[]{:S(2)}) collective-permute-start(bf16[6,128,512]{2,1,0:T(8,128)(2,1)} %get-tuple-element.38), channel_id=1, source_target_pairs={{0,1},{1,0},{2,3},{3,2},{4,5},{5,4},{6,7},{7,6},{8,9},{9,8},{10,11... | collective-permute-start | bytes 2359304 | tf_op jit(solution)/shard_map/ppermute | solution.py:419
  42.1 45.9 %collective-permute-start.6 = (bf16[4,128,512]{2,1,0:T(8,128)(2,1)}, bf16[4,128,512]{2,1,0:T(8,128)(2,1)S(1)}, u32[]{:S(2)}, u32[]{:S(2)}) collective-permute-start(bf16[4,128,512]{2,1,0:T(8,128)(2,1)} %get-tuple-element.37), channel_id=1, source_target_pairs={{0,1},{1,0},{2,3},{3,2},{4,5},{5,4},{6,7},{7,6},{8,9},{9,8},{10,11... | collective-permute-start | bytes 1572872 | tf_op jit(solution)/shard_map/ppermute | solution.py:419
  94.5 2.7 %collective-permute-start.12 = (bf16[8,16,16,256]{3,2,1,0:T(8,128)(2,1)S(1)}, bf16[8,16,16,256]{3,2,1,0:T(8,128)(2,1)S(1)}, u32[]{:S(2)}, u32[]{:S(2)}) collective-permute-start(bf16[8,16,16,256]{3,2,1,0:T(8,128)(2,1)S(1)} %get-tuple-element.60), channel_id=1, source_target_pairs={{0,2},{2,0},{4,6},{6,4},{8,10},{10,8},{12,14},{14,12},{16,18},{18,... | collective-permute-start | bytes 3145736 | tf_op jit(solution)/shard_map/ppermute | solution.py:123
  94.5 20.3 %collective-permute-start.11 = (bf16[16,48,512]{2,1,0:T(8,128)(2,1)S(1)}, bf16[16,48,512]{2,1,0:T(8,128)(2,1)S(1)}, u32[]{:S(2)}, u32[]{:S(2)}) collective-permute-start(bf16[16,48,512]{2,1,0:T(8,128)(2,1)S(1)} %get-tuple-element.58), channel_id=1, source_target_pairs={{0,1},{1,0},{2,3},{3,2},{4,5},{5,4},{6,7},{7,6},{8,9},{9,8},{10,11... | collective-permute-start | bytes 2359304 | tf_op jit(solution)/shard_map/ppermute | solution.py:419
  97.3 14.0 %collective-permute-start.13 = (bf16[4,16,16,256]{3,2,1,0:T(8,128)(2,1)S(1)}, bf16[4,16,16,256]{3,2,1,0:T(8,128)(2,1)S(1)}, u32[]{:S(2)}, u32[]{:S(2)}) collective-permute-start(bf16[4,16,16,256]{3,2,1,0:T(8,128)(2,1)S(1)} %add_convert_fusion), channel_id=1, source_target_pairs={{0,4},{2,6},{4,0},{6,2},{8,12},{10,14},{12,8},{14,10},{16,20},{18,... | collective-permute-start | bytes 1572872 | tf_op jit(solution)/shard_map/ppermute | solution.py:123
  99.1 32.6 %collective-permute-start.10 = (bf16[16,48,512]{2,1,0:T(8,128)(2,1)S(1)}, bf16[16,48,512]{2,1,0:T(8,128)(2,1)S(1)}, u32[]{:S(2)}, u32[]{:S(2)}) collective-permute-start(bf16[16,48,512]{2,1,0:T(8,128)(2,1)S(1)} %get-tuple-element.57), channel_id=1, source_target_pairs={{0,1},{1,0},{2,3},{3,2},{4,5},{5,4},{6,7},{7,6},{8,9},{9,8},{10,11... | collective-permute-start | bytes 2359304 | tf_op jit(solution)/shard_map/ppermute | solution.py:419
  120.0 3.1 %collective-permute-start.14 = (bf16[8,6,16,256]{3,2,1,0:T(8,128)(2,1)S(1)}, bf16[8,6,16,256]{3,2,1,0:T(8,128)(2,1)S(1)}, u32[]{:S(2)}, u32[]{:S(2)}) collective-permute-start(bf16[8,6,16,256]{3,2,1,0:T(8,128)(2,1)S(1)} %get-tuple-element.63), channel_id=1, source_target_pairs={{0,2},{2,0},{4,6},{6,4},{8,10},{10,8},{12,14},{14,12},{16,18},{18,... | collective-permute-start | bytes 1179656 | tf_op jit(solution)/shard_map/ppermute | solution.py:123
  120.0 27.4 %collective-permute-start.9 = (bf16[16,32,512]{2,1,0:T(8,128)(2,1)S(1)}, bf16[16,32,512]{2,1,0:T(8,128)(2,1)S(1)}, u32[]{:S(2)}, u32[]{:S(2)}) collective-permute-start(bf16[16,32,512]{2,1,0:T(8,128)(2,1)S(1)} %get-tuple-element.56), channel_id=1, source_target_pairs={{0,1},{1,0},{2,3},{3,2},{4,5},{5,4},{6,7},{7,6},{8,9},{9,8},{10,11... | collective-permute-start | bytes 1572872 | tf_op jit(solution)/shard_map/ppermute | solution.py:419
  121.6 16.9 %collective-permute-start.17 = (bf16[1,16,16,256]{3,2,1,0:T(8,128)(2,1)S(1)}, bf16[1,16,16,256]{3,2,1,0:T(8,128)(2,1)S(1)}, u32[]{:S(2)}, u32[]{:S(2)}) collective-permute-start(bf16[1,16,16,256]{3,2,1,0:T(8,128)(2,1)S(1)} %get-tuple-element.70.refs_13_), channel_id=1, source_target_pairs={{0,24},{2,26},{4,28},{6,30},{8,16},{10,18},{12,20},{14,22},{16,8},... | collective-permute-start | bytes 393224 | tf_op jit(solution)/shard_map/ppermute | solution.py:123
  123.1 15.4 %collective-permute-start.16 = (bf16[1,16,16,256]{3,2,1,0:T(8,128)(2,1)S(1)}, bf16[1,16,16,256]{3,2,1,0:T(8,128)(2,1)S(1)}, u32[]{:S(2)}, u32[]{:S(2)}) collective-permute-start(bf16[1,16,16,256]{3,2,1,0:T(8,128)(2,1)S(1)} %get-tuple-element.71.refs_12_), channel_id=1, source_target_pairs={{0,16},{2,18},{4,20},{6,22},{8,24},{10,26},{12,28},{14,30},{16,0},... | collective-permute-start | bytes 393224 | tf_op jit(solution)/shard_map/ppermute | solution.py:123
  123.1 15.4 %collective-permute-start.15 = (bf16[1,16,16,256]{3,2,1,0:T(8,128)(2,1)S(1)}, bf16[1,16,16,256]{3,2,1,0:T(8,128)(2,1)S(1)}, u32[]{:S(2)}, u32[]{:S(2)}) collective-permute-start(bf16[1,16,16,256]{3,2,1,0:T(8,128)(2,1)S(1)} %get-tuple-element.72.refs_11_), channel_id=1, source_target_pairs={{0,8},{2,10},{4,12},{6,14},{8,0},{10,2},{12,4},{14,6},{16,24},{18,... | collective-permute-start | bytes 393224 | tf_op jit(solution)/shard_map/ppermute | solution.py:123
  131.7 7.0 %collective-permute-start.18 = (bf16[4,6,16,256]{3,2,1,0:T(8,128)(2,1)S(1)}, bf16[4,6,16,256]{3,2,1,0:T(8,128)(2,1)S(1)}, u32[]{:S(2)}, u32[]{:S(2)}) collective-permute-start(bf16[4,6,16,256]{3,2,1,0:T(8,128)(2,1)S(1)} %add_convert_fusion.2.refs_12_), channel_id=1, source_target_pairs={{0,4},{2,6},{4,0},{6,2},{8,12},{10,14},{12,8},{14,10},{16,20},{18,... | collective-permute-start | bytes 589832 | tf_op jit(solution)/shard_map/ppermute | solution.py:123
  138.5 1.7 collective-permute-start.20
  138.6 12.6 %copy-start = (f32[16,16,256]{2,1,0:T(8,128)}, f32[16,16,256]{2,1,0:T(8,128)S(1)}, u32[]{:S(2)}) copy-start(f32[16,16,256]{2,1,0:T(8,128)S(1)} %multiply_bitcast_fusion.refs_12_) | copy-start | bytes 786436
  138.7 5.2 %collective-permute-start.19 = (bf16[2,6,16,256]{3,2,1,0:T(8,128)(2,1)S(1)}, bf16[2,6,16,256]{3,2,1,0:T(8,128)(2,1)S(1)}, u32[]{:S(2)}, u32[]{:S(2)}) collective-permute-start(bf16[2,6,16,256]{3,2,1,0:T(8,128)(2,1)S(1)} %add_convert_fusion.8), channel_id=1, source_target_pairs={{0,8},{2,10},{4,12},{6,14},{8,0},{10,2},{12,4},{14,6},{16,24},{18,... | collective-permute-start | bytes 294920 | tf_op jit(solution)/shard_map/ppermute | solution.py:123
  140.3 7.0 %collective-permute-start.21 = (bf16[4,6,16,256]{3,2,1,0:T(8,128)(2,1)S(1)}, bf16[4,6,16,256]{3,2,1,0:T(8,128)(2,1)S(1)}, u32[]{:S(2)}, u32[]{:S(2)}) collective-permute-start(bf16[4,6,16,256]{3,2,1,0:T(8,128)(2,1)S(1)} %add_convert_fusion.1), channel_id=1, source_target_pairs={{0,4},{2,6},{4,0},{6,2},{8,12},{10,14},{12,8},{14,10},{16,20},{18,... | collective-permute-start | bytes 589832 | tf_op jit(solution)/shard_map/ppermute | solution.py:123
  144.0 7.2 %collective-permute-start.22 = (bf16[1,6,16,256]{3,2,1,0:T(8,128)(2,1)S(1)}, bf16[1,6,16,256]{3,2,1,0:T(8,128)(2,1)S(1)}, u32[]{:S(2)}, u32[]{:S(2)}) collective-permute-start(bf16[1,6,16,256]{3,2,1,0:T(8,128)(2,1)S(1)} %add_convert_fusion.10.refs_13_), channel_id=1, source_target_pairs={{0,16},{2,18},{4,20},{6,22},{8,24},{10,26},{12,28},{14,30},{16,0},... | collective-permute-start | bytes 147464 | tf_op jit(solution)/shard_map/ppermute | solution.py:123
  151.2 1.5 collective-permute-start.25
  151.3 5.3 %collective-permute-start.23 = (bf16[2,6,16,256]{3,2,1,0:T(8,128)(2,1)S(1)}, bf16[2,6,16,256]{3,2,1,0:T(8,128)(2,1)S(1)}, u32[]{:S(2)}, u32[]{:S(2)}) collective-permute-start(bf16[2,6,16,256]{3,2,1,0:T(8,128)(2,1)S(1)} %add_convert_fusion.7.refs_14_), channel_id=1, source_target_pairs={{0,8},{2,10},{4,12},{6,14},{8,0},{10,2},{12,4},{14,6},{16,24},{18,... | collective-permute-start | bytes 294920 | tf_op jit(solution)/shard_map/ppermute | solution.py:123
  152.8 5.6 %collective-permute-start.26 = (bf16[4,4,16,256]{3,2,1,0:T(8,128)(2,1)S(1)}, bf16[4,4,16,256]{3,2,1,0:T(8,128)(2,1)S(1)}, u32[]{:S(2)}, u32[]{:S(2)}) collective-permute-start(bf16[4,4,16,256]{3,2,1,0:T(8,128)(2,1)S(1)} %add_convert_fusion.3), channel_id=1, source_target_pairs={{0,4},{2,6},{4,0},{6,2},{8,12},{10,14},{12,8},{14,10},{16,20},{18,... | collective-permute-start | bytes 393224 | tf_op jit(solution)/shard_map/ppermute | solution.py:123
  156.6 5.8 %collective-permute-start.24 = (bf16[1,6,16,256]{3,2,1,0:T(8,128)(2,1)S(1)}, bf16[1,6,16,256]{3,2,1,0:T(8,128)(2,1)S(1)}, u32[]{:S(2)}, u32[]{:S(2)}) collective-permute-start(bf16[1,6,16,256]{3,2,1,0:T(8,128)(2,1)S(1)} %add_convert_fusion.9), channel_id=1, source_target_pairs={{0,16},{2,18},{4,20},{6,22},{8,24},{10,26},{12,28},{14,30},{16,0},... | collective-permute-start | bytes 147464 | tf_op jit(solution)/shard_map/ppermute | solution.py:123
  158.4 4.1 %collective-permute-start.27 = (bf16[1,4,16,256]{3,2,1,0:T(8,128)(2,1)S(1)}, bf16[1,4,16,256]{3,2,1,0:T(8,128)(2,1)S(1)}, u32[]{:S(2)}, u32[]{:S(2)}) collective-permute-start(bf16[1,4,16,256]{3,2,1,0:T(8,128)(2,1)S(1)} %get-tuple-element.73), channel_id=1, source_target_pairs={{0,8},{2,10},{4,12},{6,14},{8,0},{10,2},{12,4},{14,6},{16,24},{18,... | collective-permute-start | bytes 98312 | tf_op jit(solution)/shard_map/ppermute | solution.py:123
  159.2 5.7 %collective-permute-start.29 = (bf16[1,4,16,256]{3,2,1,0:T(8,128)(2,1)S(1)}, bf16[1,4,16,256]{3,2,1,0:T(8,128)(2,1)S(1)}, u32[]{:S(2)}, u32[]{:S(2)}) collective-permute-start(bf16[1,4,16,256]{3,2,1,0:T(8,128)(2,1)S(1)} %get-tuple-element.74), channel_id=1, source_target_pairs={{0,24},{2,26},{4,28},{6,30},{8,16},{10,18},{12,20},{14,22},{16,8},... | collective-permute-start | bytes 98312 | tf_op jit(solution)/shard_map/ppermute | solution.py:123
  161.1 4.8 %collective-permute-start.28 = (bf16[1,4,16,256]{3,2,1,0:T(8,128)(2,1)S(1)}, bf16[1,4,16,256]{3,2,1,0:T(8,128)(2,1)S(1)}, u32[]{:S(2)}, u32[]{:S(2)}) collective-permute-start(bf16[1,4,16,256]{3,2,1,0:T(8,128)(2,1)S(1)} %get-tuple-element.75), channel_id=1, source_target_pairs={{0,16},{2,18},{4,20},{6,22},{8,24},{10,26},{12,28},{14,30},{16,0},... | collective-permute-start | bytes 98312 | tf_op jit(solution)/shard_map/ppermute | solution.py:123
Sparse Core Ops, SparseCore 0:
  10.9 49.2 all-gather.2

commit v3 on v2

--- a/solution.py
+++ b/solution.py
@@ -445,7 +445,7 @@
     net = Network(size) if cube else None
     cut = net.first_cut() if cube else [[0]]
     plain_cut = [list(range(size))] if cube else [[0]]
-    j_spans = split_by(local, (3, 3, 2)) if cube else split_even(local, 4)
+    j_spans = split_by(local, (3, 2, 2, 1)) if cube else split_even(local, 4)
     b_spans = [(2 * lo, 2 * hi) for lo, hi in split_by(local // 2, (3, 3, 2))]
     shifts = list(range(1, group))
 

time: 174 us -> 174 us (level)
  waiting for transfers between devices: 72.1 us -> 67.9 us
  Pallas kernels: 53.1 us -> 55.3 us
    ppermute x6 -> x7, waiting for transfers between devices: 12.2 us -> 9.49 us  [send(): lax.ppermute(array, 'mp', [(at, (at + shift) % group) for at in range(gro...]
    pallas_call x8 -> x9, Pallas kernels: 53.1 us -> 55.3 us  [call(): pl.pallas_call(body, grid_spec=pltpu.PrefetchScalarGridSpec(num_scalar_pr...]
    ppermute x6 -> x7, starting transfers between devices: 8.55 us -> 8.9 us  [send(): lax.ppermute(array, 'mp', [(at, (at + shift) % group) for at in range(gro...]
  transfers between devices with their start and end apart: 31 -> 32, of which waited for: 21 -> 20; matrix products, arithmetic and copies ran while one was open for 1% -> 1% of each run, Pallas kernels for 27% -> 29%
where the time goes in v3:
time: 174 us; the launch traced here: 173 us
  waiting for transfers between devices  67.9 us (39%)
  Pallas kernels  55.3 us (32%)
  starting transfers between devices  31.5 us (18%)
  between operations  14.2 us (8%)
  other arithmetic  3.33 us (2%)
    pallas_call x9, Pallas kernels, call(): pl.pallas_call(body, grid_spec=pltpu.PrefetchScalarGridSpec(num_scalar_pr...  55.3 us
    ppermute x24, waiting for transfers between devices, swap(): lax.ppermute(array, 'dp', [(at, at ^ mask) for at in range(self.size)])  42.3 us
    ppermute x24, starting transfers between devices, swap(): lax.ppermute(array, 'dp', [(at, at ^ mask) for at in range(self.size)])  22.5 us
    all_gather x1, waiting for transfers between devices, gather_plain(): whole = lax.all_gather(shard, 'dp', axis=0, tiled=False)  16.1 us
    ppermute x7, waiting for transfers between devices, send(): lax.ppermute(array, 'mp', [(at, (at + shift) % group) for at in range(gro...  9.49 us
    ppermute x7, starting transfers between devices, send(): lax.ppermute(array, 'mp', [(at, (at + shift) % group) for at in range(gro...  8.9 us
  transfers between devices with their start and end apart: 32, of which 20 were waited for; matrix products, arithmetic and copies ran while one was open for 1% of the time, Pallas kernels for 29%

profile of v3, /device:TPU:0, one launch (start us, length us, event | category | flops | bytes accessed | tf_op | source)
XLA Modules:
  0.0 173.1 jit_solution(11298893819182626889)
XLA Ops:
  7.2 0.9 dynamic-slice_bitcast_fusion
  8.1 1.6 pad_maximum_fusion.2
  9.7 5.1 %collective-permute-start.2 = (bf16[1,16,16,128]{3,2,1,0:T(8,128)(2,1)S(1)}, bf16[1,16,16,128]{3,2,1,0:T(8,128)(2,1)S(1)}, u32[]{:S(2)}, u32[]{:S(2)}) collective-permute-start(bf16[1,16,16,128]{3,2,1,0:T(8,128)(2,1)S(1)} %get-tuple-element.92), channel_id=1, source_target_pairs={{0,24},{2,26},{4,28},{6,30},{8,16},{10,18},{12,20},{14,22},{16,8},... | collective-permute-start | bytes 196616 | tf_op jit(solution)/shard_map/ppermute | solution.py:123
  14.9 0.6 collective-permute-start
  15.5 1.9 %collective-permute-done.2 = bf16[1,16,16,128]{3,2,1,0:T(8,128)(2,1)S(1)} collective-permute-done((bf16[1,16,16,128]{3,2,1,0:T(8,128)(2,1)S(1)}, bf16[1,16,16,128]{3,2,1,0:T(8,128)(2,1)S(1)}, u32[]{:S(2)}, u32[]{:S(2)}) %collective-permute-start.2) | collective-permute-done | bytes 65568 | tf_op jit(solution)/shard_map/ppermute | solution.py:123
  17.4 3.0 %collective-permute-done.1 = bf16[1,16,16,128]{3,2,1,0:T(8,128)(2,1)S(1)} collective-permute-done((bf16[1,16,16,128]{3,2,1,0:T(8,128)(2,1)S(1)}, bf16[1,16,16,128]{3,2,1,0:T(8,128)(2,1)S(1)}, u32[]{:S(2)}, u32[]{:S(2)}) %collective-permute-start.1) | collective-permute-done | bytes 65568 | tf_op jit(solution)/shard_map/ppermute | solution.py:123
  20.5 1.6 collective-permute-start.3
  22.1 8.5 %collective-permute-done.3.refs_3_.refs_8_ = bf16[4,16,16,128]{3,2,1,0:T(8,128)(2,1)S(1)} collective-permute-done((bf16[4,16,16,128]{3,2,1,0:T(8,128)(2,1)S(1)}, bf16[4,16,16,128]{3,2,1,0:T(8,128)(2,1)S(1)}, u32[]{:S(2)}, u32[]{:S(2)}) %collective-permute-start.3) | collective-permute-done | bytes 262176 | tf_op jit(solution)/shard_map/ppermute | solution.py:123
  30.6 1.5 collective-permute-done.5.refs_5_.refs_10_
  32.1 7.9 %expand.3 = (bf16[6,128,512]{2,1,0:T(8,128)(2,1)}, bf16[4,128,512]{2,1,0:T(8,128)(2,1)}, bf16[4,128,512]{2,1,0:T(8,128)(2,1)}, bf16[2,128,512]{2,1,0:T(8,128)(2,1)S(1)}) custom-call(s32[2]{0:T(128)S(1)} %pad_add_fusion.ids_ref, bf16[512,4096]{1,0:T(8,128)(2,1)} %refs_3_.13, bf16[512,4096]{1,0:T(8,128)(2,1)} %refs_3_.13, ...), custom_call_target="tpu_custom_call" | custom-call | flops 1 | bytes 1 | tf_op jit(solution)/shard_map/expand/pallas_call | solution.py:59
  40.0 1.7 collective-permute-start.9
  42.0 1.7 collective-permute-start.7
  44.0 16.1 %all-gather.3.cloned.1.call-done = bf16[256,16,384]{2,1,0:T(8,128)(2,1)} async-done(((bf16[16,16,384]{2,1,0:T(8,128)(2,1)}), bf16[256,16,384]{2,1,0:T(8,128)(2,1)}) %all-gather.3.cloned.1.call-update) | async-done | bytes 3145744 | tf_op jit(solution)/shard_map/all_gather | solution.py:424
  60.1 7.0 %expand.2.refs_0_ = bf16[16,128,512]{2,1,0:T(8,128)(2,1)S(1)} custom-call(s32[2]{0:T(128)S(1)} %pad_add_fusion.ids_ref, bf16[512,4096]{1,0:T(8,128)(2,1)} %refs_3_.13, bf16[512,4096]{1,0:T(8,128)(2,1)} %refs_3_.13, bf16[16,16,16,384]{3,2,1,0:T(8,128)(2,1)} %bitcast.13), custom_call_target="tpu_custom_call" | custom-call | flops 1 | bytes 1 | tf_op jit(solution)/shard_map/expand/pallas_call | solution.py:59
  67.1 8.7 %mix.4 = (bf16[512,4096]{1,0:T(8,128)(2,1)}, bf16[16,128,512]{2,1,0:T(8,128)(2,1)S(1)}, f32[8,16,16,256]{3,2,1,0:T(8,128)S(1)}, bf16[8,16,16,256]{3,2,1,0:T(8,12...) custom-call(s32[2]{0:T(128)S(1)} %pad_add_fusion.ids_ref, ...), custom_call_target="tpu_custom_call" | custom-call | flops 1 | bytes 1 | tf_op jit(solution)/shard_map/mix/pallas_call | solution.py:59
  75.9 6.6 %mix.5 = (bf16[512,4096]{1,0:T(8,128)(2,1)}, bf16[16,128,512]{2,1,0:T(8,128)(2,1)S(1)}, f32[8,16,16,256]{3,2,1,0:T(8,128)S(1)}, bf16[8,16,16,256]{3,2,1,0:T(8,12...) custom-call(s32[2]{0:T(128)S(1)} %pad_add_fusion.ids_ref, ...), custom_call_target="tpu_custom_call", output_to_operand_aliasing={{0}: (8, {}), {1}: (9, {}), {2}: (10, {}), {3}: (11, {}), {... | custom-call | flops 1 | bytes 1 | tf_op jit(solution)/shard_map/mix/pallas_call | solution.py:59
  83.0 6.6 %mix.6 = (bf16[512,4096]{1,0:T(8,128)(2,1)}, bf16[16,128,512]{2,1,0:T(8,128)(2,1)S(1)}, f32[8,16,16,256]{3,2,1,0:T(8,128)S(1)}, bf16[8,16,16,256]{3,2,1,0:T(8,12...) custom-call(s32[2]{0:T(128)S(1)} %pad_add_fusion.ids_ref, ...), custom_call_target="tpu_custom_call", output_to_operand_aliasing={{0}: (8, {}), {1}: (9, {}), {2}: (10, {}), {3}: (11, {}), {... | custom-call | flops 1 | bytes 1 | tf_op jit(solution)/shard_map/mix/pallas_call | solution.py:59
  89.6 4.4 %mix.7 = (bf16[512,4096]{1,0:T(8,128)(2,1)}, bf16[16,128,512]{2,1,0:T(8,128)(2,1)S(1)}, f32[8,16,16,256]{3,2,1,0:T(8,128)S(1)}, bf16[8,16,16,256]{3,2,1,0:T(8,12...) custom-call(s32[2]{0:T(128)S(1)} %pad_add_fusion.ids_ref, ...), custom_call_target="tpu_custom_call", output_to_operand_aliasing={{0}: (8, {}), {1}: (9, {}), {2}: (10, {}), {3}: (11, {}), {... | custom-call | flops 1 | bytes 1 | tf_op jit(solution)/shard_map/mix/pallas_call | solution.py:59
  94.0 1.7 collective-permute-start.12
  95.7 1.0 collective-permute-done.13
  96.9 1.7 %collective-permute-start.14 = (bf16[4,16,16,256]{3,2,1,0:T(8,128)(2,1)S(1)}, bf16[4,16,16,256]{3,2,1,0:T(8,128)(2,1)S(1)}, u32[]{:S(2)}, u32[]{:S(2)}) collective-permute-start(bf16[4,16,16,256]{3,2,1,0:T(8,128)(2,1)S(1)} %add_convert_fusion), channel_id=1, source_target_pairs={{0,4},{2,6},{4,0},{6,2},{8,12},{10,14},{12,8},{14,10},{16,20},{18,... | collective-permute-start | bytes 1572872 | tf_op jit(solution)/shard_map/ppermute | solution.py:123
  98.6 1.5 collective-permute-start.11
  100.1 10.8 %collective-permute-done.14 = bf16[4,16,16,256]{3,2,1,0:T(8,128)(2,1)S(1)} collective-permute-done((bf16[4,16,16,256]{3,2,1,0:T(8,128)(2,1)S(1)}, bf16[4,16,16,256]{3,2,1,0:T(8,128)(2,1)S(1)}, u32[]{:S(2)}, u32[]{:S(2)}) %collective-permute-start.14) | collective-permute-done | bytes 524320 | tf_op jit(solution)/shard_map/ppermute | solution.py:123
  111.1 3.3 %collective-permute-done.12.refs_1_ = bf16[16,48,512]{2,1,0:T(8,128)(2,1)S(1)} collective-permute-done((bf16[16,48,512]{2,1,0:T(8,128)(2,1)S(1)}, bf16[16,48,512]{2,1,0:T(8,128)(2,1)S(1)}, u32[]{:S(2)}, u32[]{:S(2)}) %collective-permute-start.12) | collective-permute-done | bytes 786464 | tf_op jit(solution)/shard_map/ppermute | solution.py:419
  114.4 5.1 %fold.3 = (bf16[512,4096]{1,0:T(8,128)(2,1)}, f32[8,6,16,256]{3,2,1,0:T(8,128)S(1)}, bf16[8,6,16,256]{3,2,1,0:T(8,128)(2,1)S(1)}) custom-call(s32[2]{0:T(128)S(1)} %pad_add_fusion.ids_ref, bf16[16,128,512]{2,1,0:T(8,128)(2,1)S(1)} %get-tuple-element.71.refs_0_, bf16[16,48,512]{2,1,0:T(8,128)(2,1)S(1)} %collective-permute-done.12.refs_1_, ...), custom_call_target="tpu_custom_call" | custom-call | flops 1 | bytes 1 | tf_op jit(solution)/shard_map/fold/pallas_call | solution.py:59
  119.5 1.7 collective-permute-start.10
  121.2 1.5 collective-permute-start.18
  122.7 1.3 collective-permute-start.17
  123.9 1.6 collective-permute-start.16
  125.6 5.6 %collective-permute-done.11.refs_1_ = bf16[16,48,512]{2,1,0:T(8,128)(2,1)S(1)} collective-permute-done((bf16[16,48,512]{2,1,0:T(8,128)(2,1)S(1)}, bf16[16,48,512]{2,1,0:T(8,128)(2,1)S(1)}, u32[]{:S(2)}, u32[]{:S(2)}) %collective-permute-start.11) | collective-permute-done | bytes 786464 | tf_op jit(solution)/shard_map/ppermute | solution.py:419
  131.2 1.7 collective-permute-start.19
  132.9 5.1 %fold.4 = (bf16[512,4096]{1,0:T(8,128)(2,1)}, f32[8,6,16,256]{3,2,1,0:T(8,128)S(1)}, bf16[8,6,16,256]{3,2,1,0:T(8,128)(2,1)S(1)}) custom-call(s32[2]{0:T(128)S(1)} %pad_add_fusion.ids_ref, bf16[16,128,512]{2,1,0:T(8,128)(2,1)S(1)} %get-tuple-element.71.refs_0_, ...), custom_call_target="tpu_custom_call", output_to_operand_aliasing={{0}: (12, {})} | custom-call | flops 1 | bytes 1 | tf_op jit(solution)/shard_map/fold/pallas_call | solution.py:59
  138.8 1.0 collective-permute-done.21
  140.3 3.1 %collective-permute-done.20 = bf16[2,6,16,256]{3,2,1,0:T(8,128)(2,1)S(1)} collective-permute-done((bf16[2,6,16,256]{3,2,1,0:T(8,128)(2,1)S(1)}, bf16[2,6,16,256]{3,2,1,0:T(8,128)(2,1)S(1)}, u32[]{:S(2)}, u32[]{:S(2)}) %collective-permute-start.20) | collective-permute-done | bytes 98336 | tf_op jit(solution)/shard_map/ppermute | solution.py:123
  143.5 0.7 collective-permute-start.23
  144.2 2.6 %collective-permute-done.22 = bf16[4,6,16,256]{3,2,1,0:T(8,128)(2,1)S(1)} collective-permute-done((bf16[4,6,16,256]{3,2,1,0:T(8,128)(2,1)S(1)}, bf16[4,6,16,256]{3,2,1,0:T(8,128)(2,1)S(1)}, u32[]{:S(2)}, u32[]{:S(2)}) %collective-permute-start.22) | collective-permute-done | bytes 196640 | tf_op jit(solution)/shard_map/ppermute | solution.py:123
  146.9 3.9 %fold.5 = (bf16[512,4096]{1,0:T(8,128)(2,1)}, f32[8,4,16,256]{3,2,1,0:T(8,128)S(1)}, bf16[8,4,16,256]{3,2,1,0:T(8,128)(2,1)S(1)}) custom-call(s32[2]{0:T(128)S(1)} %pad_add_fusion.ids_ref, bf16[16,128,512]{2,1,0:T(8,128)(2,1)S(1)} %get-tuple-element.71.refs_0_, ...), custom_call_target="tpu_custom_call", output_to_operand_aliasing={{0}: (12, {})} | custom-call | flops 1 | bytes 1 | tf_op jit(solution)/shard_map/fold/pallas_call | solution.py:59
  150.8 0.7 collective-permute-start.24
  151.5 0.8 collective-permute-done.26
  152.9 3.1 %collective-permute-done.24 = bf16[2,6,16,256]{3,2,1,0:T(8,128)(2,1)S(1)} collective-permute-done((bf16[2,6,16,256]{3,2,1,0:T(8,128)(2,1)S(1)}, bf16[2,6,16,256]{3,2,1,0:T(8,128)(2,1)S(1)}, u32[]{:S(2)}, u32[]{:S(2)}) %collective-permute-start.24) | collective-permute-done | bytes 98336 | tf_op jit(solution)/shard_map/ppermute | solution.py:123
  156.1 0.7 collective-permute-start.25
  156.8 1.1 collective-permute-done.27
  158.0 0.8 collective-permute-start.28
  158.7 1.9 %collective-permute-start.30 = (bf16[1,4,16,256]{3,2,1,0:T(8,128)(2,1)S(1)}, bf16[1,4,16,256]{3,2,1,0:T(8,128)(2,1)S(1)}, u32[]{:S(2)}, u32[]{:S(2)}) collective-permute-start(bf16[1,4,16,256]{3,2,1,0:T(8,128)(2,1)S(1)} %get-tuple-element.90), channel_id=1, source_target_pairs={{0,24},{2,26},{4,28},{6,30},{8,16},{10,18},{12,20},{14,22},{16,8},... | collective-permute-start | bytes 98312 | tf_op jit(solution)/shard_map/ppermute | solution.py:123
  160.7 0.9 collective-permute-start.29
  162.1 2.4 %collective-permute-done.30 = bf16[1,4,16,256]{3,2,1,0:T(8,128)(2,1)S(1)} collective-permute-done((bf16[1,4,16,256]{3,2,1,0:T(8,128)(2,1)S(1)}, bf16[1,4,16,256]{3,2,1,0:T(8,128)(2,1)S(1)}, u32[]{:S(2)}, u32[]{:S(2)}) %collective-permute-start.30) | collective-permute-done | bytes 32800 | tf_op jit(solution)/shard_map/ppermute | solution.py:123
  164.4 1.0 collective-permute-done.29
  165.5 0.7 pad_maximum_fusion.1
  (47 shorter events, 4.6 us)
Async XLA Ops:
  7.2 52.9 %all-gather.3.cloned.1.call-start = ((), (), s32[]{:S(2)}) async-start(), calls=%async_computation | async-start | bytes 3342336 | tf_op jit(solution)/shard_map/all_gather | solution.py:424
  9.7 7.7 %collective-permute-start.2 = (bf16[1,16,16,128]{3,2,1,0:T(8,128)(2,1)S(1)}, bf16[1,16,16,128]{3,2,1,0:T(8,128)(2,1)S(1)}, u32[]{:S(2)}, u32[]{:S(2)}) collective-permute-start(bf16[1,16,16,128]{3,2,1,0:T(8,128)(2,1)S(1)} %get-tuple-element.92), channel_id=1, source_target_pairs={{0,24},{2,26},{4,28},{6,30},{8,16},{10,18},{12,20},{14,22},{16,8},... | collective-permute-start | bytes 196616 | tf_op jit(solution)/shard_map/ppermute | solution.py:123
  14.9 5.6 %collective-permute-start.1 = (bf16[1,16,16,128]{3,2,1,0:T(8,128)(2,1)S(1)}, bf16[1,16,16,128]{3,2,1,0:T(8,128)(2,1)S(1)}, u32[]{:S(2)}, u32[]{:S(2)}) collective-permute-start(bf16[1,16,16,128]{3,2,1,0:T(8,128)(2,1)S(1)} %get-tuple-element.92), channel_id=1, source_target_pairs={{0,16},{2,18},{4,20},{6,22},{8,24},{10,26},{12,28},{14,30},{16,0},... | collective-permute-start | bytes 196616 | tf_op jit(solution)/shard_map/ppermute | solution.py:123
  14.9 5.6 %collective-permute-start = (bf16[1,16,16,128]{3,2,1,0:T(8,128)(2,1)S(1)}, bf16[1,16,16,128]{3,2,1,0:T(8,128)(2,1)S(1)}, u32[]{:S(2)}, u32[]{:S(2)}) collective-permute-start(bf16[1,16,16,128]{3,2,1,0:T(8,128)(2,1)S(1)} %get-tuple-element.92), channel_id=1, source_target_pairs={{0,8},{2,10},{4,12},{6,14},{8,0},{10,2},{12,4},{14,6},{16,24},{18,... | collective-permute-start | bytes 196616 | tf_op jit(solution)/shard_map/ppermute | solution.py:123
  20.5 10.0 %collective-permute-start.3 = (bf16[4,16,16,128]{3,2,1,0:T(8,128)(2,1)S(1)}, bf16[4,16,16,128]{3,2,1,0:T(8,128)(2,1)S(1)}, u32[]{:S(2)}, u32[]{:S(2)}) collective-permute-start(bf16[4,16,16,128]{3,2,1,0:T(8,128)(2,1)S(1)} %pad_maximum_fusion.refs_2_.refs_7_), channel_id=1, source_target_pairs={{0,4},{2,6},{4,0},{6,2},{8,12},{10,14},{12,8},{14,10},{16,20},{18,... | collective-permute-start | bytes 786440 | tf_op jit(solution)/shard_map/ppermute | solution.py:123
  22.1 8.6 %collective-permute-start.4 = (bf16[4,16,16,128]{3,2,1,0:T(8,128)(2,1)S(1)}, bf16[4,16,16,128]{3,2,1,0:T(8,128)(2,1)S(1)}, u32[]{:S(2)}, u32[]{:S(2)}) collective-permute-start(bf16[4,16,16,128]{3,2,1,0:T(8,128)(2,1)S(1)} %pad_maximum_fusion.refs_2_.refs_7_), channel_id=1, source_target_pairs={{0,2},{2,0},{4,6},{6,4},{8,10},{10,8},{12,14},{14,12},{16,18},{18,... | collective-permute-start | bytes 786440 | tf_op jit(solution)/shard_map/ppermute | solution.py:123
  30.6 1.5 collective-permute-start.5
  40.0 27.2 %collective-permute-start.9 = (bf16[6,128,512]{2,1,0:T(8,128)(2,1)}, bf16[6,128,512]{2,1,0:T(8,128)(2,1)S(1)}, u32[]{:S(2)}, u32[]{:S(2)}) collective-permute-start(bf16[6,128,512]{2,1,0:T(8,128)(2,1)} %get-tuple-element.48), channel_id=1, source_target_pairs={{0,1},{1,0},{2,3},{3,2},{4,5},{5,4},{6,7},{7,6},{8,9},{9,8},{10,11... | collective-permute-start | bytes 2359304 | tf_op jit(solution)/shard_map/ppermute | solution.py:419
  41.7 34.2 %collective-permute-start.8 = (bf16[4,128,512]{2,1,0:T(8,128)(2,1)}, bf16[4,128,512]{2,1,0:T(8,128)(2,1)S(1)}, u32[]{:S(2)}, u32[]{:S(2)}) collective-permute-start(bf16[4,128,512]{2,1,0:T(8,128)(2,1)} %get-tuple-element.47), channel_id=1, source_target_pairs={{0,1},{1,0},{2,3},{3,2},{4,5},{5,4},{6,7},{7,6},{8,9},{9,8},{10,11... | collective-permute-start | bytes 1572872 | tf_op jit(solution)/shard_map/ppermute | solution.py:419
  42.0 41.0 %collective-permute-start.7 = (bf16[4,128,512]{2,1,0:T(8,128)(2,1)}, bf16[4,128,512]{2,1,0:T(8,128)(2,1)S(1)}, u32[]{:S(2)}, u32[]{:S(2)}) collective-permute-start(bf16[4,128,512]{2,1,0:T(8,128)(2,1)} %get-tuple-element.46), channel_id=1, source_target_pairs={{0,1},{1,0},{2,3},{3,2},{4,5},{5,4},{6,7},{7,6},{8,9},{9,8},{10,11... | collective-permute-start | bytes 1572872 | tf_op jit(solution)/shard_map/ppermute | solution.py:419
  43.7 45.9 %collective-permute-start.6 = (bf16[2,128,512]{2,1,0:T(8,128)(2,1)S(1)}, bf16[2,128,512]{2,1,0:T(8,128)(2,1)S(1)}, u32[]{:S(2)}, u32[]{:S(2)}) collective-permute-start(bf16[2,128,512]{2,1,0:T(8,128)(2,1)S(1)} %get-tuple-element.45), channel_id=1, source_target_pairs={{0,1},{1,0},{2,3},{3,2},{4,5},{5,4},{6,7},{7,6},{8,9},{9,8},{10,11... | collective-permute-start | bytes 786440 | tf_op jit(solution)/shard_map/ppermute | solution.py:419
  94.0 2.7 %collective-permute-start.13 = (bf16[8,16,16,256]{3,2,1,0:T(8,128)(2,1)S(1)}, bf16[8,16,16,256]{3,2,1,0:T(8,128)(2,1)S(1)}, u32[]{:S(2)}, u32[]{:S(2)}) collective-permute-start(bf16[8,16,16,256]{3,2,1,0:T(8,128)(2,1)S(1)} %get-tuple-element.76), channel_id=1, source_target_pairs={{0,2},{2,0},{4,6},{6,4},{8,10},{10,8},{12,14},{14,12},{16,18},{18,... | collective-permute-start | bytes 3145736 | tf_op jit(solution)/shard_map/ppermute | solution.py:123
  94.0 20.3 %collective-permute-start.12 = (bf16[16,48,512]{2,1,0:T(8,128)(2,1)S(1)}, bf16[16,48,512]{2,1,0:T(8,128)(2,1)S(1)}, u32[]{:S(2)}, u32[]{:S(2)}) collective-permute-start(bf16[16,48,512]{2,1,0:T(8,128)(2,1)S(1)} %get-tuple-element.74), channel_id=1, source_target_pairs={{0,1},{1,0},{2,3},{3,2},{4,5},{5,4},{6,7},{7,6},{8,9},{9,8},{10,11... | collective-permute-start | bytes 2359304 | tf_op jit(solution)/shard_map/ppermute | solution.py:419
  96.9 14.0 %collective-permute-start.14 = (bf16[4,16,16,256]{3,2,1,0:T(8,128)(2,1)S(1)}, bf16[4,16,16,256]{3,2,1,0:T(8,128)(2,1)S(1)}, u32[]{:S(2)}, u32[]{:S(2)}) collective-permute-start(bf16[4,16,16,256]{3,2,1,0:T(8,128)(2,1)S(1)} %add_convert_fusion), channel_id=1, source_target_pairs={{0,4},{2,6},{4,0},{6,2},{8,12},{10,14},{12,8},{14,10},{16,20},{18,... | collective-permute-start | bytes 1572872 | tf_op jit(solution)/shard_map/ppermute | solution.py:123
  98.6 32.6 %collective-permute-start.11 = (bf16[16,48,512]{2,1,0:T(8,128)(2,1)S(1)}, bf16[16,48,512]{2,1,0:T(8,128)(2,1)S(1)}, u32[]{:S(2)}, u32[]{:S(2)}) collective-permute-start(bf16[16,48,512]{2,1,0:T(8,128)(2,1)S(1)} %get-tuple-element.73), channel_id=1, source_target_pairs={{0,1},{1,0},{2,3},{3,2},{4,5},{5,4},{6,7},{7,6},{8,9},{9,8},{10,11... | collective-permute-start | bytes 2359304 | tf_op jit(solution)/shard_map/ppermute | solution.py:419
  119.5 4.5 %collective-permute-start.15 = (bf16[8,6,16,256]{3,2,1,0:T(8,128)(2,1)S(1)}, bf16[8,6,16,256]{3,2,1,0:T(8,128)(2,1)S(1)}, u32[]{:S(2)}, u32[]{:S(2)}) collective-permute-start(bf16[8,6,16,256]{3,2,1,0:T(8,128)(2,1)S(1)} %get-tuple-element.79), channel_id=1, source_target_pairs={{0,2},{2,0},{4,6},{6,4},{8,10},{10,8},{12,14},{14,12},{16,18},{18,... | collective-permute-start | bytes 1179656 | tf_op jit(solution)/shard_map/ppermute | solution.py:123
  119.5 27.4 %collective-permute-start.10 = (bf16[16,32,512]{2,1,0:T(8,128)(2,1)S(1)}, bf16[16,32,512]{2,1,0:T(8,128)(2,1)S(1)}, u32[]{:S(2)}, u32[]{:S(2)}) collective-permute-start(bf16[16,32,512]{2,1,0:T(8,128)(2,1)S(1)} %get-tuple-element.72), channel_id=1, source_target_pairs={{0,1},{1,0},{2,3},{3,2},{4,5},{5,4},{6,7},{7,6},{8,9},{9,8},{10,11... | collective-permute-start | bytes 1572872 | tf_op jit(solution)/shard_map/ppermute | solution.py:419
  121.2 16.9 %collective-permute-start.18 = (bf16[1,16,16,256]{3,2,1,0:T(8,128)(2,1)S(1)}, bf16[1,16,16,256]{3,2,1,0:T(8,128)(2,1)S(1)}, u32[]{:S(2)}, u32[]{:S(2)}) collective-permute-start(bf16[1,16,16,256]{3,2,1,0:T(8,128)(2,1)S(1)} %get-tuple-element.86.refs_13_), channel_id=1, source_target_pairs={{0,24},{2,26},{4,28},{6,30},{8,16},{10,18},{12,20},{14,22},{16,8},... | collective-permute-start | bytes 393224 | tf_op jit(solution)/shard_map/ppermute | solution.py:123
  122.7 15.4 %collective-permute-start.17 = (bf16[1,16,16,256]{3,2,1,0:T(8,128)(2,1)S(1)}, bf16[1,16,16,256]{3,2,1,0:T(8,128)(2,1)S(1)}, u32[]{:S(2)}, u32[]{:S(2)}) collective-permute-start(bf16[1,16,16,256]{3,2,1,0:T(8,128)(2,1)S(1)} %get-tuple-element.87.refs_12_), channel_id=1, source_target_pairs={{0,16},{2,18},{4,20},{6,22},{8,24},{10,26},{12,28},{14,30},{16,0},... | collective-permute-start | bytes 393224 | tf_op jit(solution)/shard_map/ppermute | solution.py:123
  123.9 14.1 %collective-permute-start.16 = (bf16[1,16,16,256]{3,2,1,0:T(8,128)(2,1)S(1)}, bf16[1,16,16,256]{3,2,1,0:T(8,128)(2,1)S(1)}, u32[]{:S(2)}, u32[]{:S(2)}) collective-permute-start(bf16[1,16,16,256]{3,2,1,0:T(8,128)(2,1)S(1)} %get-tuple-element.88.refs_11_), channel_id=1, source_target_pairs={{0,8},{2,10},{4,12},{6,14},{8,0},{10,2},{12,4},{14,6},{16,24},{18,... | collective-permute-start | bytes 393224 | tf_op jit(solution)/shard_map/ppermute | solution.py:123
  131.2 7.0 %collective-permute-start.19 = (bf16[4,6,16,256]{3,2,1,0:T(8,128)(2,1)S(1)}, bf16[4,6,16,256]{3,2,1,0:T(8,128)(2,1)S(1)}, u32[]{:S(2)}, u32[]{:S(2)}) collective-permute-start(bf16[4,6,16,256]{3,2,1,0:T(8,128)(2,1)S(1)} %add_convert_fusion.2.refs_12_), channel_id=1, source_target_pairs={{0,4},{2,6},{4,0},{6,2},{8,12},{10,14},{12,8},{14,10},{16,20},{18,... | collective-permute-start | bytes 589832 | tf_op jit(solution)/shard_map/ppermute | solution.py:123
  138.0 1.7 collective-permute-start.21
  138.2 12.6 %copy-start = (f32[16,16,256]{2,1,0:T(8,128)}, f32[16,16,256]{2,1,0:T(8,128)S(1)}, u32[]{:S(2)}) copy-start(f32[16,16,256]{2,1,0:T(8,128)S(1)} %multiply_bitcast_fusion.refs_12_) | copy-start | bytes 786436
  138.2 5.2 %collective-permute-start.20 = (bf16[2,6,16,256]{3,2,1,0:T(8,128)(2,1)S(1)}, bf16[2,6,16,256]{3,2,1,0:T(8,128)(2,1)S(1)}, u32[]{:S(2)}, u32[]{:S(2)}) collective-permute-start(bf16[2,6,16,256]{3,2,1,0:T(8,128)(2,1)S(1)} %add_convert_fusion.8), channel_id=1, source_target_pairs={{0,8},{2,10},{4,12},{6,14},{8,0},{10,2},{12,4},{14,6},{16,24},{18,... | collective-permute-start | bytes 294920 | tf_op jit(solution)/shard_map/ppermute | solution.py:123
  139.8 7.0 %collective-permute-start.22 = (bf16[4,6,16,256]{3,2,1,0:T(8,128)(2,1)S(1)}, bf16[4,6,16,256]{3,2,1,0:T(8,128)(2,1)S(1)}, u32[]{:S(2)}, u32[]{:S(2)}) collective-permute-start(bf16[4,6,16,256]{3,2,1,0:T(8,128)(2,1)S(1)} %add_convert_fusion.1), channel_id=1, source_target_pairs={{0,4},{2,6},{4,0},{6,2},{8,12},{10,14},{12,8},{14,10},{16,20},{18,... | collective-permute-start | bytes 589832 | tf_op jit(solution)/shard_map/ppermute | solution.py:123
  143.5 7.2 %collective-permute-start.23 = (bf16[1,6,16,256]{3,2,1,0:T(8,128)(2,1)S(1)}, bf16[1,6,16,256]{3,2,1,0:T(8,128)(2,1)S(1)}, u32[]{:S(2)}, u32[]{:S(2)}) collective-permute-start(bf16[1,6,16,256]{3,2,1,0:T(8,128)(2,1)S(1)} %add_convert_fusion.10.refs_13_), channel_id=1, source_target_pairs={{0,16},{2,18},{4,20},{6,22},{8,24},{10,26},{12,28},{14,30},{16,0},... | collective-permute-start | bytes 147464 | tf_op jit(solution)/shard_map/ppermute | solution.py:123
  150.7 1.5 collective-permute-start.26
  150.8 5.3 %collective-permute-start.24 = (bf16[2,6,16,256]{3,2,1,0:T(8,128)(2,1)S(1)}, bf16[2,6,16,256]{3,2,1,0:T(8,128)(2,1)S(1)}, u32[]{:S(2)}, u32[]{:S(2)}) collective-permute-start(bf16[2,6,16,256]{3,2,1,0:T(8,128)(2,1)S(1)} %add_convert_fusion.7.refs_14_), channel_id=1, source_target_pairs={{0,8},{2,10},{4,12},{6,14},{8,0},{10,2},{12,4},{14,6},{16,24},{18,... | collective-permute-start | bytes 294920 | tf_op jit(solution)/shard_map/ppermute | solution.py:123
  152.3 5.6 %collective-permute-start.27 = (bf16[4,4,16,256]{3,2,1,0:T(8,128)(2,1)S(1)}, bf16[4,4,16,256]{3,2,1,0:T(8,128)(2,1)S(1)}, u32[]{:S(2)}, u32[]{:S(2)}) collective-permute-start(bf16[4,4,16,256]{3,2,1,0:T(8,128)(2,1)S(1)} %add_convert_fusion.3), channel_id=1, source_target_pairs={{0,4},{2,6},{4,0},{6,2},{8,12},{10,14},{12,8},{14,10},{16,20},{18,... | collective-permute-start | bytes 393224 | tf_op jit(solution)/shard_map/ppermute | solution.py:123
  156.1 5.8 %collective-permute-start.25 = (bf16[1,6,16,256]{3,2,1,0:T(8,128)(2,1)S(1)}, bf16[1,6,16,256]{3,2,1,0:T(8,128)(2,1)S(1)}, u32[]{:S(2)}, u32[]{:S(2)}) collective-permute-start(bf16[1,6,16,256]{3,2,1,0:T(8,128)(2,1)S(1)} %add_convert_fusion.9), channel_id=1, source_target_pairs={{0,16},{2,18},{4,20},{6,22},{8,24},{10,26},{12,28},{14,30},{16,0},... | collective-permute-start | bytes 147464 | tf_op jit(solution)/shard_map/ppermute | solution.py:123
  158.0 4.1 %collective-permute-start.28 = (bf16[1,4,16,256]{3,2,1,0:T(8,128)(2,1)S(1)}, bf16[1,4,16,256]{3,2,1,0:T(8,128)(2,1)S(1)}, u32[]{:S(2)}, u32[]{:S(2)}) collective-permute-start(bf16[1,4,16,256]{3,2,1,0:T(8,128)(2,1)S(1)} %get-tuple-element.89), channel_id=1, source_target_pairs={{0,8},{2,10},{4,12},{6,14},{8,0},{10,2},{12,4},{14,6},{16,24},{18,... | collective-permute-start | bytes 98312 | tf_op jit(solution)/shard_map/ppermute | solution.py:123
  158.7 5.7 %collective-permute-start.30 = (bf16[1,4,16,256]{3,2,1,0:T(8,128)(2,1)S(1)}, bf16[1,4,16,256]{3,2,1,0:T(8,128)(2,1)S(1)}, u32[]{:S(2)}, u32[]{:S(2)}) collective-permute-start(bf16[1,4,16,256]{3,2,1,0:T(8,128)(2,1)S(1)} %get-tuple-element.90), channel_id=1, source_target_pairs={{0,24},{2,26},{4,28},{6,30},{8,16},{10,18},{12,20},{14,22},{16,8},... | collective-permute-start | bytes 98312 | tf_op jit(solution)/shard_map/ppermute | solution.py:123
  160.7 4.8 %collective-permute-start.29 = (bf16[1,4,16,256]{3,2,1,0:T(8,128)(2,1)S(1)}, bf16[1,4,16,256]{3,2,1,0:T(8,128)(2,1)S(1)}, u32[]{:S(2)}, u32[]{:S(2)}) collective-permute-start(bf16[1,4,16,256]{3,2,1,0:T(8,128)(2,1)S(1)} %get-tuple-element.91), channel_id=1, source_target_pairs={{0,16},{2,18},{4,20},{6,22},{8,24},{10,26},{12,28},{14,30},{16,0},... | collective-permute-start | bytes 98312 | tf_op jit(solution)/shard_map/ppermute | solution.py:123
Sparse Core Ops, SparseCore 0:
  10.9 49.2 all-gather.2
